TPU v7x, 512 devices: a whole 4x4x16 slice. The times are simulated.
512 devices in a mesh: dp: 512 (over z, y, x, core).
Axes of the slice: x: 4, y: 4, z: 16, core: 2. Of those that a mesh axis runs over, the one named last changes fastest.
Arguments:
- attn_out: bfloat16 [65536, 1024], P('dp'), may hold values from -24 to 24
- grad_out: bfloat16 [65536, 1024], P('dp'), may hold values from -6 to 6
- w_out: bfloat16 [1024, 1024], replicated, may hold values from -0.1875 to 0.1875
- codes_m: int32 [512, 2048], P('dp'), may hold values from 0 to 254
- codes_v: int32 [512, 2048], P('dp'), may hold values from 16 to 255
- scale_m: float32 [512], P('dp'), may hold values from 0.0002 to 0.002
- scale_v: float32 [512], P('dp'), may hold values from 1e-07 to 1e-06
- master: float32 [512, 2048], P('dp'), may hold values from -0.1875 to 0.1875
Outputs:
- d_attn: bfloat16 [65536, 1024], P('dp')
- m_unit: float32 [512, 2048], P('dp')
- v_unit: float32 [512, 2048], P('dp')
- new_master: float32 [512, 2048], P('dp')
All inputs are finite; a program needn't handle non-finite values.
Results may differ from a plain program's by a relative error of at most 0.0013.
Values sent between devices are 32-bit elements; how exact they have to be, the bound alone decides.
A program may use at most 64 MiB of HBM per device.

v0:
```python
import jax
import jax.numpy as jnp
from jax import lax
from jax.sharding import PartitionSpec as P

STEP = 100


def local(attn_out, grad_out, w_out, codes_m, codes_v, scale_m, scale_v, master):
    blocks_here, block_length = codes_m.shape
    d_attn = jnp.einsum("tf,hf->th", grad_out, w_out, preferred_element_type=jnp.float32).astype(
        jnp.bfloat16
    )
    amount = lax.axis_size("dp") * blocks_here
    product = jnp.einsum(
        "th,tf->hf", attn_out, grad_out, preferred_element_type=jnp.float32
    ).reshape(-1)
    gradient = lax.psum_scatter(
        product.reshape(amount, block_length), "dp", scatter_dimension=0, tiled=True
    )
    squares = lax.psum(jnp.sum(gradient * gradient), "dp")
    clip = jnp.minimum(1.0, 1.0 / jnp.sqrt(squares + 1e-12))
    m_old = scale_m[:, None] * (codes_m.astype(jnp.float32) - 127.0) / 127.0
    ratio_v = codes_v.astype(jnp.float32) / 255.0
    v_old = scale_v[:, None] * ratio_v * ratio_v
    clipped = clip * gradient
    m_new = 0.9 * m_old + 0.1 * clipped
    v_new = 0.95 * v_old + 0.05 * clipped * clipped
    update = m_new / (1.0 - 0.9**STEP) / (jnp.sqrt(v_new / (1.0 - 0.95**STEP)) + 1e-08)
    new_master = master - 0.01 * (update + 0.1 * master)
    return (d_attn, m_new / scale_m[:, None], v_new / scale_v[:, None], new_master)


def solution(mesh):
    in_specs = (
        P("dp", None),
        P("dp", None),
        P(),
        P("dp", None),
        P("dp", None),
        P("dp"),
        P("dp"),
        P("dp", None),
    )
    out_specs = (P("dp", None), P("dp", None), P("dp", None), P("dp", None))
    return jax.shard_map(local, mesh=mesh, in_specs=in_specs, out_specs=out_specs, check_vma=False)
```

profile of v0, /device:TPU:1, one launch (start us, length us, event | category | flops | bytes accessed | tf_op | source)
XLA Modules:
  0.0 626.4 jit_solution(5322014875484479878)
XLA Ops:
  7.2 0.0 copy-start
  7.2 0.0 all-reduce.3.cloned.1.call-start
  7.2 3.9 fusion.2
  11.1 5.2 reshape_reshape.3
  16.3 0.0 copy-start.1
  16.3 0.0 copy-start.2
  16.3 0.0 copy-start.3
  16.3 0.0 copy-start.4
  16.3 0.0 all-reduce.3.cloned.1.call-update
  17.7 0.0 copy-done
  17.7 0.0 copy-done.1
  17.7 1.5 convolution_convert_fusion
  19.2 490.3 %all-reduce.3.cloned.1.call-done = f32[512,2048]{1,0:T(8,128)} async-done(((f32[512,2048]{1,0:T(8,128)}), f32[512,2048]{1,0:T(8,128)}) %all-reduce.3.cloned.1.call-update) | async-done | bytes 4194320
  509.6 1.5 multiply_reduce_fusion
  511.1 105.6 %psum.7 = f32[]{:T(128)} all-reduce(f32[]{:T(128)} %multiply_reduce_fusion), channel_id=1, replica_groups=mesh['dp'=512] {'dp'}, use_global_device_ids=true, to_apply=%region_2.0 | all-reduce | flops 1 | bytes 8 | tf_op jit(solution)/shard_map/psum | solution.py:21
  617.3 0.0 copy-done.2
  617.4 0.0 copy-done.3
  617.4 0.0 copy-done.4
  617.4 1.5 multiply_subtract_fusion
  618.9 0.6 broadcast_divide_fusion
Async XLA Ops:
  7.2 10.5 %copy-start = (bf16[1024,1024]{1,0:T(8,128)(2,1)S(1)}, bf16[1024,1024]{1,0:T(8,128)(2,1)}, u32[]{:S(2)}) copy-start(bf16[1024,1024]{1,0:T(8,128)(2,1)} %param.10) | copy-start | bytes 6291460
  7.2 502.4 %all-reduce.3.cloned.1.call-start = ((), (), s32[]{:S(2)}) async-start(), calls=%async_computation | async-start | bytes 8388608
  16.3 1.4 copy-start.1
  16.3 601.0 %copy-start.2 = (f32[1,2048]{1,0:T(1,128)S(1)}, f32[1,2048]{1,0:T(1,128)}, u32[]{:S(2)}) copy-start(f32[1,2048]{1,0:T(1,128)} %param.15) | copy-start | bytes 24580
  16.3 601.0 %copy-start.3 = (s32[1,2048]{1,0:T(1,128)S(1)}, s32[1,2048]{1,0:T(1,128)}, u32[]{:S(2)}) copy-start(s32[1,2048]{1,0:T(1,128)} %param.12) | copy-start | bytes 24580
  16.3 601.0 %copy-start.4 = (s32[1,2048]{1,0:T(1,128)S(1)}, s32[1,2048]{1,0:T(1,128)}, u32[]{:S(2)}) copy-start(s32[1,2048]{1,0:T(1,128)} %param.11) | copy-start | bytes 24580
Sparse Core Ops, SparseCore 0:
  16.5 493.0 all-reduce.2
where the time goes:
time: 627 us; the launch traced here: 626 us
  waiting for transfers between devices  490 us (78%)
  blocking collectives  106 us (17%)
  between operations  16.1 us (3%)
    unnamed x2, waiting for transfers between devices  490 us
    psum x1, blocking collectives, local(): squares = lax.psum(jnp.sum(gradient * gradient), 'dp')  106 us
  transfers between devices with their start and end apart: 1, of which 1 were waited for; matrix products, arithmetic and copies ran while one was open for 0% of the time, Pallas kernels for 0%

commit v1 on v0

v1 whole, which is shorter than its diff:
```python
import functools

import jax
import jax.numpy as jnp
from jax import lax
from jax.experimental import pallas as pl
from jax.experimental.pallas import tpu as pltpu
from jax.sharding import PartitionSpec as P

STEP = 100
NX, NY, NZ = 4, 4, 16
PLANE = NX * NY * 2
PARTS = 1
UNITS = 2 * PARTS
WIDTH = 1024 // UNITS
TOK = 128
MESH = pl.DeviceIdType.MESH


def kernel(
    a_hbm, g_hbm, w_hbm, cm_hbm, cv_hbm, sm_ref, sv_ref, ma_hbm,
    d_ref, mu_ref, vu_ref, nm_ref,
    a_in, g_in, w_in, cm, cv, ma,
    at_send, at_recv, g_send, g_recv, at_all, g_all,
    prod, first, second, zsend, zrecv, plane_sum, ring_sum,
    in_sem, core_s, core_r, first_s, first_r, second_s, second_r, z_s, z_r, p_s, p_r, q_s, q_r,
):
    me = lax.axis_index("dp")
    core = lax.rem(me, 2)
    x = lax.rem(me // 2, NX)
    y = lax.rem(me // (2 * NX), NY)
    z = me // PLANE
    q = lax.rem(me, PLANE)

    def device(z_, y_, x_, c_):
        return ((z_ * NY + y_) * NX + x_) * 2 + c_

    loads = []
    for i, (src, dst) in enumerate(
        ((a_hbm, a_in), (g_hbm, g_in), (w_hbm, w_in), (cm_hbm, cm), (cv_hbm, cv), (ma_hbm, ma))
    ):
        copy = pltpu.make_async_copy(src, dst, in_sem.at[i])
        copy.start()
        loads.append(copy)

    barrier = pltpu.get_barrier_semaphore()

    def greet_z(k, _):
        other = lax.rem(z + k, NZ)
        for c_ in range(2):
            pl.semaphore_signal(
                barrier, inc=1, device_id=(device(other, y, x, c_),), device_id_type=MESH
            )
        return 0

    def greet_plane(k, _):
        pl.semaphore_signal(
            barrier, inc=1, device_id=(z * PLANE + lax.rem(q + k, PLANE),), device_id_type=MESH
        )
        return 0

    lax.fori_loop(1, NZ, greet_z, 0)
    lax.fori_loop(1, PLANE, greet_plane, 0)

    row = lax.broadcasted_iota(jnp.int32, (512, 512), 0)
    column = lax.broadcasted_iota(jnp.int32, (512, 512), 1)
    wanted = ((row >> 2) & 7) * 64 + ((row >> 5) & 3) * 16 + ((row >> 7) & 3) * 4 + (row & 3)
    order = jnp.where(wanted == column, 1.0, 0.0).astype(jnp.bfloat16)
    loads[0].wait()
    loads[1].wait()
    for u in range(UNITS):
        piece = g_in[:, u * WIDTH : (u + 1) * WIDTH]
        g_send[u] = piece.astype(jnp.float32)
        g_all[u, 0:TOK, :] = piece

    def rows_of(c_):
        half = a_in[:, pl.ds(pl.multiple_of(c_ * 512, 512), 512)]
        return lax.dot_general(
            order, half, (((1,), (1,)), ((), ())), preferred_element_type=jnp.float32
        )

    at_send[...] = rows_of(1 - core)
    at_all[:, 0:TOK] = rows_of(core).astype(jnp.bfloat16)

    pl.semaphore_wait(barrier, (NZ - 1) * 2 + PLANE - 1)

    def push(src, dst, s, r, target):
        copy = pltpu.make_async_remote_copy(
            src_ref=src, dst_ref=dst, send_sem=s, recv_sem=r,
            device_id=(target,), device_id_type=MESH,
        )
        copy.start()
        return copy

    twin = device(z, y, x, 1 - core)
    across = [push(at_send, at_recv, core_s.at[UNITS], core_r.at[UNITS], twin)]
    for u in range(UNITS):
        across.append(push(g_send.at[u], g_recv.at[u], core_s.at[u], core_r.at[u], twin))
    across[0].wait_recv()
    at_all[:, TOK : 2 * TOK] = at_recv[...].astype(jnp.bfloat16)

    def block(u, k):
        if u % 2 == 0:
            rows = at_all[pl.ds(pl.multiple_of(k * 128, 128), 128), :]
        else:
            rows = jnp.concatenate(
                [at_all[pl.ds(pl.multiple_of(i * 128 + k * 32, 32), 32), :] for i in range(4)],
                axis=0,
            )
        return jnp.dot(rows, g_all[u], preferred_element_type=jnp.float32)

    def places(u):
        return (x, y) if u % 2 == 0 else (y, x)

    def along(u, stage, k):
        if (u % 2 == 0) == (stage == 0):
            return device(z, y, k, core)
        return device(z, k, x, core)

    sent_first = {}
    for u in range(UNITS):
        across[u + 1].wait_recv()
        g_all[u, TOK : 2 * TOK, :] = g_recv[u].astype(jnp.bfloat16)
    for s in range(PARTS):
        for hop in (2, 1, 3):
            for u in (2 * s, 2 * s + 1):
                k = lax.rem(places(u)[0] + hop, 4)
                prod[u, hop] = block(u, k)
                sent_first[u, hop] = push(
                    prod.at[u, hop], first.at[u, hop - 1],
                    first_s.at[u, hop - 1], first_r.at[u, hop - 1], along(u, 0, k),
                )
        for u in (2 * s, 2 * s + 1):
            prod[u, 0] = block(u, places(u)[0])

    loads[2].wait()
    for h in range(4):
        d_ref[:, h * 256 : (h + 1) * 256] = lax.dot_general(
            g_in[...], w_in[h * 256 : (h + 1) * 256, :], (((1,), (1,)), ((), ())),
            preferred_element_type=jnp.float32,
        ).astype(jnp.bfloat16)

    sent_second = {}
    for u in range(UNITS):
        for hop in (1, 3, 2):
            sent_first[u, hop].wait_recv()
        total = prod[u, 0] + first[u, 0] + first[u, 1] + first[u, 2]
        prod[u, 0] = total
        for hop in (2, 1, 3):
            k = lax.rem(places(u)[1] + hop, 4)
            sent_second[u, hop] = push(
                prod.at[u, 0, pl.ds(pl.multiple_of(k * 32, 32), 32)], second.at[u, hop - 1],
                second_s.at[u, hop - 1], second_r.at[u, hop - 1], along(u, 1, k),
            )

    for u in range(UNITS):
        for hop in (1, 3, 2):
            sent_second[u, hop].wait_recv()
        mine = prod[u, 0, pl.ds(pl.multiple_of(places(u)[1] * 32, 32), 32)]
        total = mine + second[u, 0] + second[u, 1] + second[u, 2]
        for k in range(16):
            zsend[k, :, u * WIDTH : (u + 1) * WIDTH] = total[2 * k : 2 * k + 2]

    def z_copy(k):
        z_, c_ = 8 * core + k // 2, lax.rem(k, 2)
        return z_, c_, pltpu.make_async_remote_copy(
            src_ref=zsend.at[k], dst_ref=zrecv.at[z], send_sem=z_s, recv_sem=z_r,
            device_id=(device(z_, y, x, c_),), device_id_type=MESH,
        )

    def z_start(i, _):
        k = lax.rem(i + 2 * z + 8, 16)
        z_, c_, copy = z_copy(k)
        mine = jnp.logical_and(z_ == z, c_ == core)

        @pl.when(jnp.logical_not(mine))
        def _():
            copy.start()

        @pl.when(mine)
        def _():
            pltpu.make_async_copy(zsend.at[k], zrecv.at[z], z_r).start()

        return 0

    lax.fori_loop(0, 16, z_start, 0)
    pltpu.make_async_copy(zrecv, zrecv, z_r).wait()
    gradient = zrecv[0]
    for k in range(1, NZ):
        gradient = gradient + zrecv[k]

    def spread(slots, slot, count, target, s, r, value):
        slots[slot] = jnp.full((1, 128), value, jnp.float32)

        def start(k, _):
            pltpu.make_async_remote_copy(
                src_ref=slots.at[slot], dst_ref=slots.at[slot], send_sem=s, recv_sem=r,
                device_id=(target(k),), device_id_type=MESH,
            ).start()
            return 0

        lax.fori_loop(1, count, start, 0)
        arrived = slots.at[pl.ds(0, count - 1)]
        pltpu.make_async_copy(arrived, arrived, r).wait()
        return jnp.sum(slots[...], axis=0)

    square = jnp.sum(gradient * gradient)
    square = spread(
        plane_sum, q, PLANE, lambda k: z * PLANE + lax.rem(q + k, PLANE), p_s, p_r, square
    )[0, 0]
    square = spread(
        ring_sum, z, NZ, lambda k: lax.rem(z + k, NZ) * PLANE + q, q_s, q_r, square
    )
    clip = jnp.minimum(1.0, 1.0 / jnp.sqrt(square[:, 0:1] + 1e-12))

    for load in loads[3:]:
        load.wait()
    scale_m, scale_v = sm_ref[0], sv_ref[0]
    for p in range(2):
        part = slice(p * 1024, (p + 1) * 1024)
        m_old = scale_m * (cm[:, part].astype(jnp.float32) - 127.0) / 127.0
        ratio_v = cv[:, part].astype(jnp.float32) / 255.0
        v_old = scale_v * ratio_v * ratio_v
        clipped = clip * gradient[p : p + 1, :]
        m_new = 0.9 * m_old + 0.1 * clipped
        v_new = 0.95 * v_old + 0.05 * clipped * clipped
        update = m_new / (1.0 - 0.9**STEP) / (jnp.sqrt(v_new / (1.0 - 0.95**STEP)) + 1e-08)
        nm_ref[:, part] = ma[:, part] - 0.01 * (update + 0.1 * ma[:, part])
        mu_ref[:, part] = m_new / scale_m
        vu_ref[:, part] = v_new / scale_v

    for copy in across:
        copy.wait_send()
    for copy in (*sent_first.values(), *sent_second.values()):
        copy.wait_send()
    away = jnp.logical_not((z // 8) == core)

    @pl.when(away)
    def _():
        pltpu.make_async_copy(zsend, zsend, z_s).wait()

    @pl.when(jnp.logical_not(away))
    def _():
        left = zsend.at[pl.ds(0, 15)]
        pltpu.make_async_copy(left, left, z_s).wait()

    for slots, count, s in ((plane_sum, PLANE, p_s), (ring_sum, NZ, q_s)):
        left = slots.at[pl.ds(0, count - 1)]
        pltpu.make_async_copy(left, left, s).wait()


def local(attn_out, grad_out, w_out, codes_m, codes_v, scale_m, scale_v, master):
    f32, bf16 = jnp.float32, jnp.bfloat16
    vmem, dma = pltpu.VMEM, pltpu.SemaphoreType.DMA
    block = jax.ShapeDtypeStruct((1, 2048), f32)
    anywhere = pl.BlockSpec(memory_space=pl.ANY)
    scalar = pl.BlockSpec(memory_space=pltpu.SMEM)
    return pl.pallas_call(
        kernel,
        out_shape=(jax.ShapeDtypeStruct((TOK, 1024), bf16), block, block, block),
        in_specs=[anywhere] * 5 + [scalar] * 2 + [anywhere],
        out_specs=tuple([pl.BlockSpec(memory_space=pltpu.VMEM)] * 4),
        scratch_shapes=[
            vmem((TOK, 1024), bf16),
            vmem((TOK, 1024), bf16),
            vmem((1024, 1024), bf16),
            vmem((1, 2048), jnp.int32),
            vmem((1, 2048), jnp.int32),
            vmem((1, 2048), f32),
            vmem((512, TOK), f32),
            vmem((512, TOK), f32),
            vmem((UNITS, TOK, WIDTH), f32),
            vmem((UNITS, TOK, WIDTH), f32),
            vmem((512, 2 * TOK), bf16),
            vmem((UNITS, 2 * TOK, WIDTH), bf16),
            vmem((UNITS, 4, 128, WIDTH), f32),
            vmem((UNITS, 3, 128, WIDTH), f32),
            vmem((UNITS, 3, 32, WIDTH), f32),
            vmem((16, 2, 1024), f32),
            vmem((NZ, 2, 1024), f32),
            vmem((PLANE, 1, 128), f32),
            vmem((NZ, 1, 128), f32),
            dma((6,)),
            dma((UNITS + 1,)),
            dma((UNITS + 1,)),
            dma((UNITS, 3)),
            dma((UNITS, 3)),
            dma((UNITS, 3)),
            dma((UNITS, 3)),
            dma,
            dma,
            dma,
            dma,
            dma,
            dma,
        ],
        compiler_params=pltpu.CompilerParams(
            collective_id=0, has_side_effects=True, vmem_limit_bytes=40 * 2**20
        ),
        cost_estimate=pl.CostEstimate(
            flops=2 * 2 * TOK * 1024 * 1024, bytes_accessed=3 * 2**20, transcendentals=4096
        ),
    )(attn_out, grad_out, w_out, codes_m, codes_v, scale_m, scale_v, master)


def solution(mesh):
    in_specs = (
        P("dp", None),
        P("dp", None),
        P(),
        P("dp", None),
        P("dp", None),
        P("dp"),
        P("dp"),
        P("dp", None),
    )
    out_specs = (P("dp", None), P("dp", None), P("dp", None), P("dp", None))
    return jax.shard_map(local, mesh=mesh, in_specs=in_specs, out_specs=out_specs, check_vma=False)
```

time: 627 us -> 71.2 us (0.11)
  waiting for transfers between devices: 490 us -> 0 us
  blocking collectives: 106 us -> 0 us
  Pallas kernels: 0 us -> 60.9 us
  between operations: 16.1 us -> 1.95 us
    unnamed x2 -> x0, waiting for transfers between devices: 490 us -> none
    psum x1 -> x0, blocking collectives: 106 us -> none  [local(): squares = lax.psum(jnp.sum(gradient * gradient), 'dp')]
    pallas_call x0 -> x1, Pallas kernels: none -> 60.9 us  [local(): pl.pallas_call(kernel, out_shape=(jax.ShapeDtypeStruct((TOK, 1024), bf16)...]
    unnamed x10 -> x16, local copies, waits for them, and re-layouts: 0.02 us -> 8.07 us
  transfers between devices with their start and end apart: 1 -> 0, of which waited for: 1 -> 0; matrix products, arithmetic and copies ran while one was open for 0% -> 0% of each run, Pallas kernels for 0% -> 0%
where the time goes in v1:
time: 71.2 us; the launch traced here: 70.9 us
  Pallas kernels  60.9 us (86%)
  local copies, waits for them, and re-layouts  8.07 us (11%)
  between operations  1.95 us (3%)
    pallas_call x1, Pallas kernels, local(): pl.pallas_call(kernel, out_shape=(jax.ShapeDtypeStruct((TOK, 1024), bf16)...  60.9 us
    unnamed x16, local copies, waits for them, and re-layouts  8.07 us

profile of v1, /device:TPU:1, one launch (start us, length us, event | category | flops | bytes accessed | tf_op | source)
XLA Modules:
  0.0 70.9 jit_solution(4636178962532003765)
XLA Ops:
  1.9 0.0 copy-start
  1.9 1.6 %copy-done = bf16[1024,1024]{1,0:T(8,128)(2,1)S(1)} copy-done((bf16[1024,1024]{1,0:T(8,128)(2,1)S(1)}, bf16[1024,1024]{1,0:T(8,128)(2,1)}, u32[]{:S(2)}) %copy-start) | copy-done | bytes 2097176
  3.5 0.0 copy-start.1
  3.5 0.9 %copy-done.1 = bf16[128,1024]{1,0:T(8,128)(2,1)S(1)} copy-done((bf16[128,1024]{1,0:T(8,128)(2,1)S(1)}, bf16[128,1024]{1,0:T(8,128)(2,1)}, u32[]{:S(2)}) %copy-start.1) | copy-done | bytes 262168
  4.5 0.0 copy-start.2
  4.5 0.9 %copy-done.2 = bf16[128,1024]{1,0:T(8,128)(2,1)S(1)} copy-done((bf16[128,1024]{1,0:T(8,128)(2,1)S(1)}, bf16[128,1024]{1,0:T(8,128)(2,1)}, u32[]{:S(2)}) %copy-start.2) | copy-done | bytes 262168
  5.4 0.0 copy-start.3
  5.4 0.7 copy-done.3
  6.1 0.0 copy-start.4
  6.1 0.7 copy-done.4
  6.8 0.0 copy-start.5
  6.8 0.7 copy-done.5
  7.5 60.9 %shard_map.111 = (bf16[128,1024]{1,0:T(8,128)(2,1)S(1)}, f32[1,2048]{1,0:T(1,128)S(1)}, f32[1,2048]{1,0:T(1,128)S(1)}, f32[1,2048]{1,0:T(1,128)S(1)}) custom-call(bf16[128,1024]{1,0:T(8,128)(2,1)S(1)} %copy-done.1, bf16[128,1024]{1,0:T(8,128)(2,1)S(1)} %copy-done.2, bf16[1024,1024]{1,0:T(8,128)(2,1)S(1)} %copy-done, s32[1,2048]{1,0:T(1,128)S(1)} %copy-done.3, ...), custom_call_target="tpu_custom_call" | custom-call | flops 536870912 | bytes 3145728 | tf_op jit(solution)/shard_map/pallas_call | solution.py:258
  68.4 0.7 copy.18
  69.1 0.6 copy.19
  69.7 0.6 copy.20
  70.3 0.6 copy.21
Async XLA Ops:
  1.9 1.6 %copy-start = (bf16[1024,1024]{1,0:T(8,128)(2,1)S(1)}, bf16[1024,1024]{1,0:T(8,128)(2,1)}, u32[]{:S(2)}) copy-start(bf16[1024,1024]{1,0:T(8,128)(2,1)} %w_hbm.1) | copy-start | bytes 6291460
  3.5 0.9 %copy-start.1 = (bf16[128,1024]{1,0:T(8,128)(2,1)S(1)}, bf16[128,1024]{1,0:T(8,128)(2,1)}, u32[]{:S(2)}) copy-start(bf16[128,1024]{1,0:T(8,128)(2,1)} %a_hbm.1) | copy-start | bytes 786436
  4.5 0.9 %copy-start.2 = (bf16[128,1024]{1,0:T(8,128)(2,1)S(1)}, bf16[128,1024]{1,0:T(8,128)(2,1)}, u32[]{:S(2)}) copy-start(bf16[128,1024]{1,0:T(8,128)(2,1)} %g_hbm.1) | copy-start | bytes 786436
  5.4 0.7 copy-start.3
  6.1 0.7 copy-start.4
  6.8 0.7 copy-start.5

commit v2 on v0

v2 whole, which is shorter than its diff:
```python
import functools

import jax
import jax.numpy as jnp
from jax import lax
from jax.experimental import pallas as pl
from jax.experimental.pallas import tpu as pltpu
from jax.sharding import PartitionSpec as P

STEP = 100
NX, NY, NZ = 4, 4, 16
PLANE = NX * NY * 2
TOK = 128
WIDTHS = (256, 256, 256, 256)
STARTS = tuple(sum(WIDTHS[:u]) for u in range(4))
PLAIN, PAIRED = (0, 1), (2, 3)
WIDE0, WIDE1 = WIDTHS[0] + WIDTHS[1], WIDTHS[2] + WIDTHS[3]
HOPS = (2, 1, 3)
MESH = pl.DeviceIdType.MESH


def push(src, dst, s, r, target):
    copy = pltpu.make_async_remote_copy(
        src_ref=src, dst_ref=dst, send_sem=s, recv_sem=r, device_id=(target,), device_id_type=MESH
    )
    copy.start()
    return copy


def kernel(
    a_hbm, g_hbm, w_hbm, cm_hbm, cv_hbm, ma_hbm,
    d_ref, gradient_ref, square_ref, cm_ref, cv_ref, ma_ref,
    a_in, g_in, w_in,
    at_send, at_recv, g_send, g_recv, at_all, g_all,
    prod0, prod1, prod2, prod3, pair, pair_in, first_in, first_in_p, second_in, second_in_p,
    zsend0, zrecv0, zsend1, zrecv1, plane_sum, ring_sum,
    in_sem, core_s, core_r, pair_s, pair_r, first_s, first_r, second_s, second_r,
    z0_s, z0_r, z1_s, z1_r, p_s, p_r, q_s, q_r,
):
    me = lax.axis_index("dp")
    core = lax.rem(me, 2)
    x = lax.rem(me // 2, NX)
    y = lax.rem(me // (2 * NX), NY)
    z = me // PLANE
    q = lax.rem(me, PLANE)
    parity = lax.rem(z, 2)

    def device(z_, y_, x_, c_):
        return ((z_ * NY + y_) * NX + x_) * 2 + c_

    loads = []
    for i, (src, dst) in enumerate(
        (
            (a_hbm, a_in), (g_hbm, g_in), (w_hbm, w_in),
            (cm_hbm, cm_ref), (cv_hbm, cv_ref), (ma_hbm, ma_ref),
        )
    ):
        copy = pltpu.make_async_copy(src, dst, in_sem.at[i])
        copy.start()
        loads.append(copy)

    barrier = pltpu.get_barrier_semaphore()

    def greet_z(k, _):
        other = lax.rem(z + k + 7, NZ)

        @pl.when(other != z)
        def _():
            for c_ in range(2):
                pl.semaphore_signal(
                    barrier, inc=1, device_id=(device(other, y, x, c_),), device_id_type=MESH
                )

        return 0

    def greet_plane(k, _):
        pl.semaphore_signal(
            barrier, inc=1, device_id=(z * PLANE + lax.rem(q + k, PLANE),), device_id_type=MESH
        )
        return 0

    lax.fori_loop(0, NZ, greet_z, 0)
    lax.fori_loop(1, PLANE, greet_plane, 0)

    row = lax.broadcasted_iota(jnp.int32, (512, 512), 0)
    column = lax.broadcasted_iota(jnp.int32, (512, 512), 1)
    wanted = (
        ((row >> 2) & 3) * 128
        + ((row >> 4) & 1) * 64
        + ((row >> 5) & 3) * 16
        + ((row >> 7) & 3) * 4
        + (row & 3)
    )
    order = jnp.where(wanted == column, 1.0, 0.0).astype(jnp.bfloat16)

    def rows_of(c_):
        half = a_in[:, pl.ds(pl.multiple_of(c_ * 512, 512), 512)]
        return lax.dot_general(
            order, half, (((1,), (1,)), ((), ())), preferred_element_type=jnp.float32
        )

    loads[0].wait()
    at_send[...] = rows_of(1 - core)
    loads[1].wait()
    for u in range(4):
        piece = g_in[:, STARTS[u] : STARTS[u] + 256]
        g_send[u] = piece.astype(jnp.float32)

    pl.semaphore_wait(barrier, (NZ - 1) * 2 + PLANE - 1)

    twin = device(z, y, x, 1 - core)
    across = {4: push(at_send, at_recv, core_s.at[4], core_r.at[4], twin)}
    for u in (*PAIRED, *PLAIN):
        across[u] = push(g_send.at[u], g_recv.at[u], core_s.at[u], core_r.at[u], twin)

    at_all[:, :, :, :, 0:TOK] = rows_of(core).astype(jnp.bfloat16).reshape(4, 4, 2, 16, TOK)
    for u in range(4):
        g_all[u, 0:TOK, :] = g_in[:, STARTS[u] : STARTS[u] + 256]
    across[4].wait_recv()
    at_all[:, :, :, :, TOK : 2 * TOK] = (
        at_recv[...].astype(jnp.bfloat16).reshape(4, 4, 2, 16, TOK)
    )

    def times(rows, u):
        return jnp.dot(rows, g_all[u], preferred_element_type=jnp.float32)

    def block(u, k):
        rows = at_all[k] if u % 2 == 0 else at_all[:, k]
        return times(rows.reshape(128, 2 * TOK), u).reshape(4, 32, WIDTHS[u])

    def block_of(u, k, parity_):
        rows = at_all[k, :, parity_] if u % 2 == 0 else at_all[:, k, parity_]
        return times(rows.reshape(64, 2 * TOK), u).reshape(4, 16, WIDTHS[u])

    def places(u):
        return (x, y) if u % 2 == 0 else (y, x)

    def along(u, stage, k):
        if (u % 2 == 0) == (stage == 0):
            return device(z, y, k, core)
        return device(z, k, x, core)

    prod = (prod0, prod1, prod2, prod3)
    step = 1 - 2 * parity
    mates = {
        2: device(lax.rem(z + step + NZ, NZ), y, x, core),
        3: device(lax.rem(z - step + NZ, NZ), y, x, core),
    }
    sent_pair, sent_first, sent_second = {}, {}, {}

    def send_first(u, hop):
        k = lax.rem(places(u)[0] + hop, 4)
        into = first_in if u in PLAIN else first_in_p
        sent_first[u, hop] = push(
            prod[u].at[hop], into.at[u % 2, hop - 1],
            first_s.at[u, hop - 1], first_r.at[u, hop - 1], along(u, 0, k),
        )

    for u in (*PAIRED, *PLAIN):
        across[u].wait_recv()
        g_all[u, TOK : 2 * TOK, :] = g_recv[u].astype(jnp.bfloat16)
    for hop in (*HOPS, 0):
        for u in PAIRED:
            k = lax.rem(places(u)[0] + hop, 4)
            pair[u - 2, hop] = block_of(u, k, 1 - parity)
            sent_pair[u, hop] = push(
                pair.at[u - 2, hop], pair_in.at[u - 2, hop],
                pair_s.at[u - 2, hop], pair_r.at[u - 2, hop], mates[u],
            )
        if hop:
            for u in PLAIN:
                prod[u][hop] = block(u, lax.rem(places(u)[0] + hop, 4))
                send_first(u, hop)
    for hop in (*HOPS, 0):
        for u in PAIRED:
            prod[u][hop] = block_of(u, lax.rem(places(u)[0] + hop, 4), parity)
    for u in PLAIN:
        prod[u][0] = block(u, places(u)[0])

    def cotangent(h):
        d_ref[:, h * 256 : (h + 1) * 256] = lax.dot_general(
            g_in[...], w_in[h * 256 : (h + 1) * 256, :], (((1,), (1,)), ((), ())),
            preferred_element_type=jnp.float32,
        ).astype(jnp.bfloat16)

    for hop in HOPS:
        for u in PAIRED:
            sent_pair[u, hop].wait_recv()
            prod[u][hop] = prod[u][hop] + pair_in[u - 2, hop]
            send_first(u, hop)

    loads[2].wait()
    for h in range(4):
        cotangent(h)

    def end_first(u):
        into = first_in if u in PLAIN else first_in_p
        if u in PAIRED:
            sent_pair[u, 0].wait_recv()
        for hop in (1, 3, 2):
            sent_first[u, hop].wait_recv()
        i = u % 2
        total = prod[u][0] + into[i, 0] + into[i, 1] + into[i, 2]
        if u in PAIRED:
            total = total + pair_in[u - 2, 0]
        prod[u][0] = total
        into = second_in if u in PLAIN else second_in_p
        for hop in HOPS:
            k = lax.rem(places(u)[1] + hop, 4)
            sent_second[u, hop] = push(
                prod[u].at[0, k], into.at[i, hop - 1],
                second_s.at[u, hop - 1], second_r.at[u, hop - 1], along(u, 1, k),
            )

    def end_second(u, zsend):
        into = second_in if u in PLAIN else second_in_p
        for hop in (1, 3, 2):
            sent_second[u, hop].wait_recv()
        i = u % 2
        total = prod[u][0, places(u)[1]] + into[i, 0] + into[i, 1] + into[i, 2]
        start = STARTS[u] - STARTS[u - i]
        for k in range(zsend.shape[0]):
            zsend[k, :, start : start + WIDTHS[u]] = total[2 * k : 2 * k + 2]

    def along_z(zsend, zrecv, s, r, slot, count, owner):
        def start(i, _):
            k, z_, c_ = owner(i)
            mine = jnp.logical_and(z_ == z, c_ == core)

            @pl.when(jnp.logical_not(mine))
            def _():
                push(zsend.at[k], zrecv.at[slot], s, r, device(z_, y, x, c_))

            @pl.when(mine)
            def _():
                pltpu.make_async_copy(zsend.at[k], zrecv.at[slot], r).start()

            return 0

        lax.fori_loop(0, count, start, 0)

    def owner0(i):
        near, c_ = lax.rem(z + 4 + i // 2, 8), lax.rem(i, 2)
        return lax.rem(near, 2) * 8 + (near // 2) * 2 + c_, 8 * core + near, c_

    def owner1(i):
        near, c_ = lax.rem(z // 2 + 2 + i // 2, 4), lax.rem(i, 2)
        return near * 2 + c_, 8 * core + 2 * near + parity, c_

    for u in PLAIN:
        end_first(u)
    for u in PAIRED:
        end_first(u)
    for u in PLAIN:
        end_second(u, zsend0)
    along_z(zsend0, zrecv0, z0_s, z0_r, z, 16, owner0)
    for u in PAIRED:
        end_second(u, zsend1)
    along_z(zsend1, zrecv1, z1_s, z1_r, z // 2, 8, owner1)

    def gather_z(zrecv, r):
        pltpu.make_async_copy(zrecv, zrecv, r).wait()
        total = zrecv[0]
        for k in range(1, zrecv.shape[0]):
            total = total + zrecv[k]
        return total

    plain = gather_z(zrecv0, z0_r)
    gradient_ref[:, 0:WIDE0] = plain
    paired = gather_z(zrecv1, z1_r)
    gradient_ref[:, WIDE0:1024] = paired

    def spread(slots, slot, count, target, s, r, value):
        slots[slot] = jnp.full((1, 128), value, jnp.float32)

        def start(k, _):
            push(slots.at[slot], slots.at[slot], s, r, target(k))
            return 0

        lax.fori_loop(1, count, start, 0)
        arrived = slots.at[pl.ds(0, count - 1)]
        pltpu.make_async_copy(arrived, arrived, r).wait()
        return jnp.sum(slots[...], axis=0)

    square = jnp.sum(plain * plain) + jnp.sum(paired * paired)
    square = spread(
        plane_sum, q, PLANE, lambda k: z * PLANE + lax.rem(q + k, PLANE), p_s, p_r, square
    )[0, 0]
    square_ref[...] = spread(
        ring_sum, z, NZ, lambda k: lax.rem(z + k + 7 + k // 9, NZ) * PLANE + q, q_s, q_r, square
    )

    for load in loads[3:]:
        load.wait()
    for sent in (across, sent_pair, sent_first, sent_second):
        for copy in sent.values():
            copy.wait_send()

    def left(buffer, count, s):
        gone = buffer.at[pl.ds(0, count)]
        pltpu.make_async_copy(gone, gone, s).wait()

    at_home = (z // 8) == core

    @pl.when(at_home)
    def _():
        left(zsend0, 15, z0_s)
        left(zsend1, 7, z1_s)

    @pl.when(jnp.logical_not(at_home))
    def _():
        left(zsend0, 16, z0_s)
        left(zsend1, 8, z1_s)

    left(plane_sum, PLANE - 1, p_s)
    left(ring_sum, NZ - 1, q_s)


def update_kernel(
    d_ref, gradient_ref, square_ref, cm, cv, ma, sm_ref, sv_ref,
    d_out, mu_out, vu_out, nm_out,
    mu, vu, nm, sem,
):
    stores = [
        pltpu.make_async_copy(src, dst, sem.at[i])
        for i, (src, dst) in enumerate(((d_ref, d_out), (mu, mu_out), (vu, vu_out), (nm, nm_out)))
    ]
    stores[0].start()
    clip = jnp.minimum(1.0, 1.0 / jnp.sqrt(square_ref[:, 0:1] + 1e-12))
    scale_m, scale_v = sm_ref[0], sv_ref[0]
    for p in range(2):
        part = slice(p * 1024, (p + 1) * 1024)
        m_old = scale_m * (cm[:, part].astype(jnp.float32) - 127.0) / 127.0
        ratio_v = cv[:, part].astype(jnp.float32) / 255.0
        v_old = scale_v * ratio_v * ratio_v
        clipped = clip * gradient_ref[p : p + 1, :]
        m_new = 0.9 * m_old + 0.1 * clipped
        v_new = 0.95 * v_old + 0.05 * clipped * clipped
        update = m_new / (1.0 - 0.9**STEP) / (jnp.sqrt(v_new / (1.0 - 0.95**STEP)) + 1e-08)
        nm[:, part] = ma[:, part] - 0.01 * (update + 0.1 * ma[:, part])
        mu[:, part] = m_new / scale_m
        vu[:, part] = v_new / scale_v
    for store in stores[1:]:
        store.start()
    for store in stores:
        store.wait()


def local(attn_out, grad_out, w_out, codes_m, codes_v, scale_m, scale_v, master):
    f32, bf16 = jnp.float32, jnp.bfloat16
    vmem, dma = pltpu.VMEM, pltpu.SemaphoreType.DMA
    shape = jax.ShapeDtypeStruct
    hbm = pl.BlockSpec(memory_space=pltpu.HBM)
    near = pl.BlockSpec(memory_space=pltpu.VMEM)
    scalar = pl.BlockSpec(memory_space=pltpu.SMEM)
    integers = shape((1, 2048), jnp.int32)
    block = shape((1, 2048), f32)
    near_by = pl.pallas_call(
        kernel,
        out_shape=(
            shape((TOK, 1024), bf16), shape((2, 1024), f32), shape((1, 128), f32),
            integers, integers, block,
        ),
        in_specs=[hbm] * 6,
        out_specs=(near,) * 6,
        scratch_shapes=[
            vmem((TOK, 1024), bf16),
            vmem((TOK, 1024), bf16),
            vmem((1024, 1024), bf16),
            vmem((512, TOK), f32),
            vmem((512, TOK), f32),
            vmem((4, TOK, 256), f32),
            vmem((4, TOK, 256), f32),
            vmem((4, 4, 2, 16, 2 * TOK), bf16),
            vmem((4, 2 * TOK, 256), bf16),
            vmem((4, 4, 32, WIDTHS[0]), f32),
            vmem((4, 4, 32, WIDTHS[1]), f32),
            vmem((4, 4, 16, WIDTHS[2]), f32),
            vmem((4, 4, 16, WIDTHS[3]), f32),
            vmem((2, 4, 4, 16, WIDTHS[2]), f32),
            vmem((2, 4, 4, 16, WIDTHS[2]), f32),
            vmem((2, 3, 4, 32, WIDTHS[0]), f32),
            vmem((2, 3, 4, 16, WIDTHS[2]), f32),
            vmem((2, 3, 32, WIDTHS[0]), f32),
            vmem((2, 3, 16, WIDTHS[2]), f32),
            vmem((16, 2, WIDE0), f32),
            vmem((16, 2, WIDE0), f32),
            vmem((8, 2, WIDE1), f32),
            vmem((8, 2, WIDE1), f32),
            vmem((PLANE, 1, 128), f32),
            vmem((NZ, 1, 128), f32),
            dma((6,)),
            dma((5,)),
            dma((5,)),
            dma((2, 4)),
            dma((2, 4)),
            dma((4, 3)),
            dma((4, 3)),
            dma((4, 3)),
            dma((4, 3)),
            *[dma] * 8,
        ],
        compiler_params=pltpu.CompilerParams(
            collective_id=0, has_side_effects=True, vmem_limit_bytes=60 * 2**20
        ),
        cost_estimate=pl.CostEstimate(
            flops=2 * 2 * TOK * 1024 * 1024, bytes_accessed=3 * 2**20, transcendentals=0
        ),
    )(attn_out, grad_out, w_out, codes_m, codes_v, master)
    return pl.pallas_call(
        update_kernel,
        out_shape=(shape((TOK, 1024), bf16), block, block, block),
        in_specs=[near] * 6 + [scalar] * 2,
        out_specs=(hbm,) * 4,
        scratch_shapes=[
            vmem((1, 2048), f32),
            vmem((1, 2048), f32),
            vmem((1, 2048), f32),
            dma((4,)),
        ],
        cost_estimate=pl.CostEstimate(flops=2048 * 30, bytes_accessed=2**19, transcendentals=4096),
    )(*near_by, scale_m, scale_v)


def solution(mesh):
    in_specs = (
        P("dp", None),
        P("dp", None),
        P(),
        P("dp", None),
        P("dp", None),
        P("dp"),
        P("dp"),
        P("dp", None),
    )
    out_specs = (P("dp", None), P("dp", None), P("dp", None), P("dp", None))
    return jax.shard_map(local, mesh=mesh, in_specs=in_specs, out_specs=out_specs, check_vma=False)
```

time: 627 us -> 58.2 us (0.09)
  waiting for transfers between devices: 490 us -> 0 us
  blocking collectives: 106 us -> 0 us
  Pallas kernels: 0 us -> 56.1 us
  between operations: 16.1 us -> 1.93 us
    unnamed x2 -> x0, waiting for transfers between devices: 490 us -> none
    psum x1 -> x0, blocking collectives: 106 us -> none  [local(): squares = lax.psum(jnp.sum(gradient * gradient), 'dp')]
    pallas_call x0 -> x2, Pallas kernels: none -> 56.1 us  [the longest x1 54.4 us: local(): pl.pallas_call(kernel, out_shape=(shape((TOK, 1024), bf16), shape((2, 102...]
  transfers between devices with their start and end apart: 1 -> 0, of which waited for: 1 -> 0; matrix products, arithmetic and copies ran while one was open for 0% -> 0% of each run, Pallas kernels for 0% -> 0%
where the time goes in v2:
time: 58.2 us; the launch traced here: 58.1 us
  Pallas kernels  56.1 us (96%)
  between operations  1.93 us (3%)
    pallas_call x1, Pallas kernels, local(): pl.pallas_call(kernel, out_shape=(shape((TOK, 1024), bf16), shape((2, 102...  54.4 us
    pallas_call x1, Pallas kernels, local(): pl.pallas_call(update_kernel, out_shape=(shape((TOK, 1024), bf16), block,...  1.74 us

profile of v2, /device:TPU:1, one launch (start us, length us, event | category | flops | bytes accessed | tf_op | source)
XLA Modules:
  0.0 58.1 jit_solution(6543010761312363565)
XLA Ops:
  1.9 54.4 %shard_map.111 = (bf16[128,1024]{1,0:T(8,128)(2,1)}, f32[2,1024]{1,0:T(2,128)}, f32[1,128]{1,0:T(1,128)}, s32[1,2048]{1,0:T(1,128)}, s32[1,2048]{1,0:T(1,128)}, /*index=5*/f32[1,2048]{1,0:T(1,128)}) custom-call(bf16[128,1024]{1,0:T(8,128)(2,1)} %a_hbm.1, bf16[128,1024]{1,0:T(8,128)(2,1)} %g_hbm.1, bf16[1024,1024]{1,0:T(8,128)(2,1)} %w_hbm.1, ...), custom_call_target="tpu_custom_call" | custom-call | flops 536870912 | bytes 3145728 | tf_op jit(solution)/shard_map/pallas_call | solution.py:358
  56.3 1.7 %shard_map.112 = (bf16[128,1024]{1,0:T(8,128)(2,1)}, f32[1,2048]{1,0:T(1,128)}, f32[1,2048]{1,0:T(1,128)}, f32[1,2048]{1,0:T(1,128)}) custom-call(bf16[128,1024]{1,0:T(8,128)(2,1)} %get-tuple-element.10.d_ref, f32[2,1024]{1,0:T(2,128)} %get-tuple-element.11.gradient_ref, f32[1,128]{1,0:T(1,128)} %get-tuple-element.12.square_ref, ...), custom_call_target="tpu_custom_call" | custom-call | flops 61440 | bytes 524288 | tf_op jit(solution)/shard_map/pallas_call | solution.py:410

commit v3 on v2

v3 whole, which is shorter than its diff:
```python
import functools

import jax
import jax.numpy as jnp
from jax import lax
from jax.experimental import pallas as pl
from jax.experimental.pallas import tpu as pltpu
from jax.sharding import PartitionSpec as P

STEP = 100
NX, NY, NZ = 4, 4, 16
PLANE = NX * NY * 2
TOK = 128
WIDTHS = (256, 256, 256, 256)
STARTS = tuple(sum(WIDTHS[:u]) for u in range(4))
PLAIN, PAIRED = (0, 1), (2, 3)
WIDE0, WIDE1 = WIDTHS[0] + WIDTHS[1], WIDTHS[2] + WIDTHS[3]
HOPS = (2, 1, 3)
MESH = pl.DeviceIdType.MESH


def push(src, dst, s, r, target):
    copy = pltpu.make_async_remote_copy(
        src_ref=src, dst_ref=dst, send_sem=s, recv_sem=r, device_id=(target,), device_id_type=MESH
    )
    copy.start()
    return copy


def wrap(value, n):
    return jnp.where(value >= n, value - n, value)


def kernel(
    a_hbm, g_hbm, w_hbm,
    d_hbm, result_hbm,
    d_ref, result, a_in, g_in, w_in,
    at_send, at_recv, g_send, g_recv, at_all, g_all,
    prod0, prod1, prod2, prod3, pair, pair_in, first_in, first_in_p, second_in, second_in_p,
    zsend0, zrecv0, zsend1, zrecv1, plane_sum, ring_sum,
    in_sem, core_s, core_r, pair_s, pair_r, first_s, first_r, second_s, second_r,
    z0_s, z0_r, z1_s, z1_r, p_s, p_r, q_s, q_r, d_sem, result_sem,
    order, near1, near2, near4, near_twin,
):
    me = lax.axis_index("dp")
    core = lax.rem(me, 2)
    x = lax.rem(me // 2, NX)
    y = lax.rem(me // (2 * NX), NY)
    z = me // PLANE
    q = lax.rem(me, PLANE)
    parity = lax.rem(z, 2)

    def device(z_, y_, x_, c_):
        return ((z_ * NY + y_) * NX + x_) * 2 + c_

    loads = []
    for i, (src, dst) in enumerate(((a_hbm, a_in), (g_hbm, g_in), (w_hbm, w_in))):
        copy = pltpu.make_async_copy(src, dst, in_sem.at[i])
        copy.start()
        loads.append(copy)

    def up(k):
        return device(wrap(z + k, NZ), y, x, core)

    def signal(semaphore, *targets):
        for target in targets:
            pl.semaphore_signal(
                semaphore, inc=1, device_id=(target,), device_id_type=MESH
            )

    twin = device(z, y, x, 1 - core)
    signal(
        pltpu.get_barrier_semaphore(), up(1), up(NZ - 1),
        *[device(z, y, wrap(x + k, NX), core) for k in HOPS],
        *[device(z, wrap(y + k, NY), x, core) for k in HOPS],
        twin,
    )

    row = lax.broadcasted_iota(jnp.int32, (512, 512), 0)
    column = lax.broadcasted_iota(jnp.int32, (512, 512), 1)
    wanted = (
        ((row >> 2) & 3) * 128
        + ((row >> 4) & 1) * 64
        + ((row >> 5) & 3) * 16
        + ((row >> 7) & 3) * 4
        + (row & 3)
    )
    order[...] = jnp.where(wanted == column, 1.0, 0.0).astype(jnp.bfloat16)

    def rows_of(c_):
        half = a_in[:, pl.ds(pl.multiple_of(c_ * 512, 512), 512)]
        return lax.dot_general(
            order[...], half, (((1,), (1,)), ((), ())), preferred_element_type=jnp.float32
        )

    loads[0].wait()
    at_send[...] = rows_of(1 - core)
    loads[1].wait()
    for u in range(4):
        piece = g_in[:, STARTS[u] : STARTS[u] + 256]
        g_send[u] = piece.astype(jnp.float32)

    pl.semaphore_wait(pltpu.get_barrier_semaphore(), 9)

    across = {4: push(at_send, at_recv, core_s.at[4], core_r.at[4], twin)}
    for u in (*PLAIN, *PAIRED):
        across[u] = push(g_send.at[u], g_recv.at[u], core_s.at[u], core_r.at[u], twin)
    signal(near1, up(1), up(NZ - 1))

    at_all[:, :, :, :, 0:TOK] = rows_of(core).astype(jnp.bfloat16).reshape(4, 4, 2, 16, TOK)
    for u in range(4):
        g_all[u, 0:TOK, :] = g_in[:, STARTS[u] : STARTS[u] + 256]
    across[4].wait_recv()
    at_all[:, :, :, :, TOK : 2 * TOK] = (
        at_recv[...].astype(jnp.bfloat16).reshape(4, 4, 2, 16, TOK)
    )

    def times(rows, u):
        return jnp.dot(rows, g_all[u], preferred_element_type=jnp.float32)

    def block(u, k):
        rows = at_all[k] if u % 2 == 0 else at_all[:, k]
        return times(rows.reshape(128, 2 * TOK), u).reshape(4, 32, WIDTHS[u])

    def block_of(u, k, parity_):
        rows = at_all[k, :, parity_] if u % 2 == 0 else at_all[:, k, parity_]
        return times(rows.reshape(64, 2 * TOK), u).reshape(4, 16, WIDTHS[u])

    def places(u):
        return (x, y) if u % 2 == 0 else (y, x)

    def along(u, stage, k):
        if (u % 2 == 0) == (stage == 0):
            return device(z, y, k, core)
        return device(z, k, x, core)

    prod = (prod0, prod1, prod2, prod3)
    odd = parity == 1
    mates = {
        2: jnp.where(odd, up(NZ - 1), up(1)),
        3: jnp.where(odd, up(1), up(NZ - 1)),
    }
    sent_pair, sent_first, sent_second = {}, {}, {}

    def send_first(u, hop):
        k = wrap(places(u)[0] + hop, 4)
        into = first_in if u in PLAIN else first_in_p
        sent_first[u, hop] = push(
            prod[u].at[hop], into.at[u % 2, hop - 1],
            first_s.at[u, hop - 1], first_r.at[u, hop - 1], along(u, 0, k),
        )

    def start_plain(u, hop):
        prod[u][hop] = block(u, wrap(places(u)[0] + hop, 4))
        send_first(u, hop)

    def start_paired(u, hop):
        pair[u - 2, hop] = block_of(u, wrap(places(u)[0] + hop, 4), 1 - parity)
        sent_pair[u, hop] = push(
            pair.at[u - 2, hop], pair_in.at[u - 2, hop],
            pair_s.at[u - 2, hop], pair_r.at[u - 2, hop], mates[u],
        )

    for hop in (*HOPS, 0):
        for u in range(4):
            if hop == HOPS[0]:
                across[u].wait_recv()
                g_all[u, TOK : 2 * TOK, :] = g_recv[u].astype(jnp.bfloat16)
            if u in PAIRED:
                start_paired(u, hop)
            elif hop:
                start_plain(u, hop)
    for hop in (*HOPS, 0):
        for u in PAIRED:
            prod[u][hop] = block_of(u, wrap(places(u)[0] + hop, 4), parity)
    for u in PLAIN:
        prod[u][0] = block(u, places(u)[0])

    def cotangent(h):
        d_ref[:, h * 256 : (h + 1) * 256] = lax.dot_general(
            g_in[...], w_in[h * 256 : (h + 1) * 256, :], (((1,), (1,)), ((), ())),
            preferred_element_type=jnp.float32,
        ).astype(jnp.bfloat16)

    for hop in HOPS:
        for u in PAIRED:
            sent_pair[u, hop].wait_recv()
            prod[u][hop] = prod[u][hop] + pair_in[u - 2, hop]
            send_first(u, hop)

    pl.semaphore_wait(near1, 2)
    signal(near2, up(2), up(NZ - 2))
    loads[2].wait()
    for h in range(4):
        cotangent(h)
    d_store = pltpu.make_async_copy(d_ref, d_hbm, d_sem)
    d_store.start()
    pl.semaphore_wait(near2, 2)
    signal(near4, up(4), up(NZ - 4))

    def end_first(u):
        into = first_in if u in PLAIN else first_in_p
        if u in PAIRED:
            sent_pair[u, 0].wait_recv()
        for hop in (1, 3, 2):
            sent_first[u, hop].wait_recv()
        i = u % 2
        total = prod[u][0] + into[i, 0] + into[i, 1] + into[i, 2]
        if u in PAIRED:
            total = total + pair_in[u - 2, 0]
        prod[u][0] = total
        into = second_in if u in PLAIN else second_in_p
        for hop in HOPS:
            k = wrap(places(u)[1] + hop, 4)
            sent_second[u, hop] = push(
                prod[u].at[0, k], into.at[i, hop - 1],
                second_s.at[u, hop - 1], second_r.at[u, hop - 1], along(u, 1, k),
            )

    def end_second(u, zsend):
        into = second_in if u in PLAIN else second_in_p
        for hop in (1, 3, 2):
            sent_second[u, hop].wait_recv()
        i = u % 2
        total = prod[u][0, places(u)[1]] + into[i, 0] + into[i, 1] + into[i, 2]
        start = STARTS[u] - STARTS[u - i]
        for k in range(zsend.shape[0]):
            to = k if u in PAIRED else (k % 8 // 2 * 2 + k // 8) * 2 + k % 2
            zsend[to, :, start : start + WIDTHS[u]] = total[2 * k : 2 * k + 2]

    def along_z(zsend, zrecv, s, r, slot, near, count, z_of):
        for offset in sorted(range(count), key=lambda k: -min(k, count - k)):
            place = wrap(near + offset, count)
            z_ = z_of(place)
            for c_ in (core, 1 - core):
                k = place * 2 + c_
                if offset == 0 and c_ is core:
                    mine = z_ == z

                    @pl.when(jnp.logical_not(mine))
                    def _():
                        push(zsend.at[k], zrecv.at[slot], s, r, device(z_, y, x, c_))

                    @pl.when(mine)
                    def _():
                        pltpu.make_async_copy(zsend.at[k], zrecv.at[slot], r).start()
                else:
                    push(zsend.at[k], zrecv.at[slot], s, r, device(z_, y, x, c_))

    for u in PLAIN:
        end_first(u)
    pl.semaphore_wait(near4, 2)
    signal(near_twin, twin)
    for u in PAIRED:
        end_first(u)
    for u in PLAIN:
        end_second(u, zsend0)
    pl.semaphore_wait(near_twin, 1)
    along_z(
        zsend0, zrecv0, z0_s, z0_r, z, lax.rem(z, 8), 8, lambda place: 8 * core + place
    )
    for u in PAIRED:
        end_second(u, zsend1)
    along_z(
        zsend1, zrecv1, z1_s, z1_r, z // 2, lax.rem(z // 2, 4), 4,
        lambda place: 8 * core + 2 * place + parity,
    )

    def gather_z(zrecv, r):
        pltpu.make_async_copy(zrecv, zrecv, r).wait()
        total = zrecv[0]
        for k in range(1, zrecv.shape[0]):
            total = total + zrecv[k]
        return total

    plain = gather_z(zrecv0, z0_r)
    result[0:2, 0:WIDE0] = plain
    paired = gather_z(zrecv1, z1_r)
    result[0:2, WIDE0:1024] = paired

    def spread(slots, slot, count, first, wrapped, target, s, r, value):
        slots[slot] = value

        def start(k, _):
            push(slots.at[slot], slots.at[slot], s, r, target(wrapped(k)))
            return 0

        lax.fori_loop(first, first + count - 1, start, 0)
        arrived = slots.at[pl.ds(0, count - 1)]
        pltpu.make_async_copy(arrived, arrived, r).wait()
        return jnp.sum(slots[...], axis=0)

    square = jnp.zeros((1, 128), jnp.float32)
    for part in (plain, paired):
        lanes = jnp.sum(part * part, axis=0, keepdims=True)
        for k in range(part.shape[1] // 128):
            square = square + lanes[:, k * 128 : (k + 1) * 128]
    base = z * PLANE
    square = spread(
        plane_sum, q, PLANE, 1, lambda k: wrap(q + k, PLANE), lambda k: base + k, p_s, p_r, square
    )
    result[2:3, 0:128] = spread(
        ring_sum, z, NZ, 8, lambda k: wrap(wrap(z + k + jnp.where(k >= NZ, 1, 0), NZ), NZ),
        lambda k: k * PLANE + q, q_s, q_r, square,
    )

    store = pltpu.make_async_copy(result, result_hbm, result_sem)
    store.start()
    store.wait()
    d_store.wait()
    for sent in (across, sent_pair, sent_first, sent_second):
        for copy in sent.values():
            copy.wait_send()

    def left(buffer, count, s):
        gone = buffer.at[pl.ds(0, count)]
        pltpu.make_async_copy(gone, gone, s).wait()

    at_home = (z // 8) == core

    @pl.when(at_home)
    def _():
        left(zsend0, 15, z0_s)
        left(zsend1, 7, z1_s)

    @pl.when(jnp.logical_not(at_home))
    def _():
        left(zsend0, 16, z0_s)
        left(zsend1, 8, z1_s)

    left(plane_sum, PLANE - 1, p_s)
    left(ring_sum, NZ - 1, q_s)


def update_kernel(
    d_hbm, result_hbm, cm_hbm, cv_hbm, ma_hbm, sm_hbm, sv_hbm,
    d_out, mu_out, vu_out, nm_out,
    result, cm, cv, ma, sm, sv, mu, vu, nm, d, load_sem, store_sem,
):
    stores = [
        pltpu.make_async_copy(src, dst, store_sem.at[i])
        for i, (src, dst) in enumerate(((d, d_out), (mu, mu_out), (vu, vu_out), (nm, nm_out)))
    ]
    loads = [
        pltpu.make_async_copy(src, dst, load_sem.at[i])
        for i, (src, dst) in enumerate(
            (
                (result_hbm, result), (cm_hbm, cm), (cv_hbm, cv), (ma_hbm, ma),
                (sm_hbm, sm), (sv_hbm, sv), (d_hbm, d),
            )
        )
    ]
    for load in loads:
        load.start()
    for load in loads[:-1]:
        load.wait()
    squares = jnp.sum(result[2:3, 0:128], axis=1, keepdims=True)
    clip = jnp.minimum(1.0, 1.0 / jnp.sqrt(squares + 1e-12))
    scale_m, scale_v = sm[0], sv[0]
    for p in range(2):
        part = slice(p * 1024, (p + 1) * 1024)
        m_old = scale_m * (cm[:, part].astype(jnp.float32) - 127.0) / 127.0
        ratio_v = cv[:, part].astype(jnp.float32) / 255.0
        v_old = scale_v * ratio_v * ratio_v
        clipped = clip * result[p : p + 1, :]
        m_new = 0.9 * m_old + 0.1 * clipped
        v_new = 0.95 * v_old + 0.05 * clipped * clipped
        update = m_new / (1.0 - 0.9**STEP) / (jnp.sqrt(v_new / (1.0 - 0.95**STEP)) + 1e-08)
        nm[:, part] = ma[:, part] - 0.01 * (update + 0.1 * ma[:, part])
        mu[:, part] = m_new / scale_m
        vu[:, part] = v_new / scale_v
    for store in stores[1:]:
        store.start()
    loads[-1].wait()
    stores[0].start()
    for store in stores:
        store.wait()


def local(attn_out, grad_out, w_out, codes_m, codes_v, scale_m, scale_v, master):
    f32, bf16 = jnp.float32, jnp.bfloat16
    vmem, dma = pltpu.VMEM, pltpu.SemaphoreType.DMA
    shape = jax.ShapeDtypeStruct
    hbm = pl.BlockSpec(memory_space=pltpu.HBM)
    block = shape((1, 2048), f32)
    d_attn, result = pl.pallas_call(
        kernel,
        out_shape=(shape((TOK, 1024), bf16), shape((4, 1024), f32)),
        in_specs=[hbm] * 3,
        out_specs=(hbm,) * 2,
        scratch_shapes=[
            vmem((TOK, 1024), bf16),
            vmem((4, 1024), f32),
            vmem((TOK, 1024), bf16),
            vmem((TOK, 1024), bf16),
            vmem((1024, 1024), bf16),
            vmem((512, TOK), f32),
            vmem((512, TOK), f32),
            vmem((4, TOK, 256), f32),
            vmem((4, TOK, 256), f32),
            vmem((4, 4, 2, 16, 2 * TOK), bf16),
            vmem((4, 2 * TOK, 256), bf16),
            vmem((4, 4, 32, WIDTHS[0]), f32),
            vmem((4, 4, 32, WIDTHS[1]), f32),
            vmem((4, 4, 16, WIDTHS[2]), f32),
            vmem((4, 4, 16, WIDTHS[3]), f32),
            vmem((2, 4, 4, 16, WIDTHS[2]), f32),
            vmem((2, 4, 4, 16, WIDTHS[2]), f32),
            vmem((2, 3, 4, 32, WIDTHS[0]), f32),
            vmem((2, 3, 4, 16, WIDTHS[2]), f32),
            vmem((2, 3, 32, WIDTHS[0]), f32),
            vmem((2, 3, 16, WIDTHS[2]), f32),
            vmem((16, 2, WIDE0), f32),
            vmem((16, 2, WIDE0), f32),
            vmem((8, 2, WIDE1), f32),
            vmem((8, 2, WIDE1), f32),
            vmem((PLANE, 1, 128), f32),
            vmem((NZ, 1, 128), f32),
            dma((3,)),
            dma((5,)),
            dma((5,)),
            dma((2, 4)),
            dma((2, 4)),
            dma((4, 3)),
            dma((4, 3)),
            dma((4, 3)),
            dma((4, 3)),
            *[dma] * 10,
            vmem((512, 512), bf16),
            *[pltpu.SemaphoreType.REGULAR] * 4,
        ],
        compiler_params=pltpu.CompilerParams(
            collective_id=0, has_side_effects=True, vmem_limit_bytes=60 * 2**20
        ),
        cost_estimate=pl.CostEstimate(
            flops=2 * 2 * TOK * 1024 * 1024, bytes_accessed=3 * 2**20, transcendentals=0
        ),
    )(attn_out, grad_out, w_out)
    return pl.pallas_call(
        update_kernel,
        out_shape=(shape((TOK, 1024), bf16), block, block, block),
        in_specs=[hbm] * 7,
        out_specs=(hbm,) * 4,
        scratch_shapes=[
            vmem((4, 1024), f32),
            vmem((1, 2048), jnp.int32),
            vmem((1, 2048), jnp.int32),
            vmem((1, 2048), f32),
            pltpu.SMEM((1,), f32),
            pltpu.SMEM((1,), f32),
            vmem((1, 2048), f32),
            vmem((1, 2048), f32),
            vmem((1, 2048), f32),
            vmem((TOK, 1024), bf16),
            dma((7,)),
            dma((4,)),
        ],
        compiler_params=pltpu.CompilerParams(vmem_limit_bytes=60 * 2**20),
        cost_estimate=pl.CostEstimate(flops=2048 * 30, bytes_accessed=2**19, transcendentals=4096),
    )(d_attn, result, codes_m, codes_v, master, scale_m, scale_v)


def solution(mesh):
    in_specs = (
        P("dp", None),
        P("dp", None),
        P(),
        P("dp", None),
        P("dp", None),
        P("dp"),
        P("dp"),
        P("dp", None),
    )
    out_specs = (P("dp", None), P("dp", None), P("dp", None), P("dp", None))
    return jax.shard_map(local, mesh=mesh, in_specs=in_specs, out_specs=out_specs, check_vma=False)
```

time: 58.2 us -> 54.8 us (0.942)
  Pallas kernels: 56.1 us -> 52.6 us
    pallas_call x1, Pallas kernels: 54.4 us -> 50.8 us  [local(): pl.pallas_call(kernel, out_shape=(shape((TOK, 1024), bf16), shape((4, 102...]
where the time goes in v3:
time: 54.8 us; the launch traced here: 54.5 us
  Pallas kernels  52.6 us (96%)
  between operations  1.93 us (4%)
    pallas_call x1, Pallas kernels, local(): pl.pallas_call(kernel, out_shape=(shape((TOK, 1024), bf16), shape((4, 102...  50.8 us
    pallas_call x1, Pallas kernels, local(): pl.pallas_call(update_kernel, out_shape=(shape((TOK, 1024), bf16), block,...  1.82 us

profile of v3, /device:TPU:1, one launch (start us, length us, event | category | flops | bytes accessed | tf_op | source)
XLA Modules:
  0.0 54.5 jit_solution(15713404586877779819)
XLA Ops:
  1.9 50.8 %shard_map.111 = (bf16[128,1024]{1,0:T(8,128)(2,1)}, f32[4,1024]{1,0:T(4,128)}) custom-call(bf16[128,1024]{1,0:T(8,128)(2,1)} %a_hbm.1, bf16[128,1024]{1,0:T(8,128)(2,1)} %g_hbm.1, bf16[1024,1024]{1,0:T(8,128)(2,1)} %w_hbm.1), custom_call_target="tpu_custom_call" | custom-call | flops 536870912 | bytes 3145728 | tf_op jit(solution)/shard_map/pallas_call | solution.py:386
  52.7 1.8 %shard_map.112 = (bf16[128,1024]{1,0:T(8,128)(2,1)}, f32[1,2048]{1,0:T(1,128)}, f32[1,2048]{1,0:T(1,128)}, f32[1,2048]{1,0:T(1,128)}) custom-call(bf16[128,1024]{1,0:T(8,128)(2,1)} %get-tuple-element.6.d_hbm, f32[4,1024]{1,0:T(4,128)} %get-tuple-element.7.result_hbm, s32[1,2048]{1,0:T(1,128)} %cm_hbm.1, s32[1,2048]{1,0:T(1,128)} %cv_hbm.1, ...), custom_call_target="tpu_custom_call" | custom-call | flops 61440 | bytes 524288 | tf_op jit(solution)/shard_map/pallas_call | solution.py:439

commit v4 on v3

--- a/solution.py
+++ b/solution.py
@@ -35,7 +35,8 @@
     a_hbm, g_hbm, w_hbm,
     d_hbm, result_hbm,
     d_ref, result, a_in, g_in, w_in,
-    at_send, at_recv, g_send, g_recv, at_all, g_all,
+    at_send, at_recv, at_all,
+    gs0, gs1, gs2, gs3, gr0, gr1, gr2, gr3, ga0, ga1, ga2, ga3,
     prod0, prod1, prod2, prod3, pair, pair_in, first_in, first_in_p, second_in, second_in_p,
     zsend0, zrecv0, zsend1, zrecv1, plane_sum, ring_sum,
     in_sem, core_s, core_r, pair_s, pair_r, first_s, first_r, second_s, second_r,
@@ -54,7 +55,7 @@
         return ((z_ * NY + y_) * NX + x_) * 2 + c_
 
     loads = []
-    for i, (src, dst) in enumerate(((a_hbm, a_in), (g_hbm, g_in), (w_hbm, w_in))):
+    for i, (src, dst) in enumerate(((g_hbm, g_in), (a_hbm, a_in), (w_hbm, w_in))):
         copy = pltpu.make_async_copy(src, dst, in_sem.at[i])
         copy.start()
         loads.append(copy)
@@ -93,30 +94,35 @@
             order[...], half, (((1,), (1,)), ((), ())), preferred_element_type=jnp.float32
         )
 
+    g_send, g_recv, g_all = (gs0, gs1, gs2, gs3), (gr0, gr1, gr2, gr3), (ga0, ga1, ga2, ga3)
+    across = {}
+
+    def cross(u):
+        piece = g_in[:, STARTS[u] : STARTS[u] + WIDTHS[u]]
+        g_send[u][...] = piece.astype(jnp.float32)
+        if u == 0:
+            pl.semaphore_wait(pltpu.get_barrier_semaphore(), 9)
+        across[u] = push(g_send[u], g_recv[u], core_s.at[u], core_r.at[u], twin)
+        g_all[u][0:TOK, :] = piece
+
     loads[0].wait()
+    for u in PLAIN:
+        cross(u)
+    loads[1].wait()
     at_send[...] = rows_of(1 - core)
-    loads[1].wait()
-    for u in range(4):
-        piece = g_in[:, STARTS[u] : STARTS[u] + 256]
-        g_send[u] = piece.astype(jnp.float32)
-
-    pl.semaphore_wait(pltpu.get_barrier_semaphore(), 9)
-
-    across = {4: push(at_send, at_recv, core_s.at[4], core_r.at[4], twin)}
-    for u in (*PLAIN, *PAIRED):
-        across[u] = push(g_send.at[u], g_recv.at[u], core_s.at[u], core_r.at[u], twin)
+    across[4] = push(at_send, at_recv, core_s.at[4], core_r.at[4], twin)
+    for u in PAIRED:
+        cross(u)
     signal(near1, up(1), up(NZ - 1))
 
     at_all[:, :, :, :, 0:TOK] = rows_of(core).astype(jnp.bfloat16).reshape(4, 4, 2, 16, TOK)
-    for u in range(4):
-        g_all[u, 0:TOK, :] = g_in[:, STARTS[u] : STARTS[u] + 256]
     across[4].wait_recv()
     at_all[:, :, :, :, TOK : 2 * TOK] = (
         at_recv[...].astype(jnp.bfloat16).reshape(4, 4, 2, 16, TOK)
     )
 
     def times(rows, u):
-        return jnp.dot(rows, g_all[u], preferred_element_type=jnp.float32)
+        return jnp.dot(rows, g_all[u][...], preferred_element_type=jnp.float32)
 
     def block(u, k):
         rows = at_all[k] if u % 2 == 0 else at_all[:, k]
@@ -165,11 +171,14 @@
         for u in range(4):
             if hop == HOPS[0]:
                 across[u].wait_recv()
-                g_all[u, TOK : 2 * TOK, :] = g_recv[u].astype(jnp.bfloat16)
+                g_all[u][TOK : 2 * TOK, :] = g_recv[u][...].astype(jnp.bfloat16)
             if u in PAIRED:
                 start_paired(u, hop)
             elif hop:
                 start_plain(u, hop)
+        if hop == HOPS[0]:
+            pl.semaphore_wait(near1, 2)
+            signal(near2, up(2), up(NZ - 2))
     for hop in (*HOPS, 0):
         for u in PAIRED:
             prod[u][hop] = block_of(u, wrap(places(u)[0] + hop, 4), parity)
@@ -182,21 +191,21 @@
             preferred_element_type=jnp.float32,
         ).astype(jnp.bfloat16)
 
+    pl.semaphore_wait(near2, 2)
+    signal(near4, up(4), up(NZ - 4))
     for hop in HOPS:
         for u in PAIRED:
             sent_pair[u, hop].wait_recv()
             prod[u][hop] = prod[u][hop] + pair_in[u - 2, hop]
             send_first(u, hop)
 
-    pl.semaphore_wait(near1, 2)
-    signal(near2, up(2), up(NZ - 2))
     loads[2].wait()
     for h in range(4):
         cotangent(h)
     d_store = pltpu.make_async_copy(d_ref, d_hbm, d_sem)
     d_store.start()
-    pl.semaphore_wait(near2, 2)
-    signal(near4, up(4), up(NZ - 4))
+    pl.semaphore_wait(near4, 2)
+    signal(near_twin, twin)
 
     def end_first(u):
         into = first_in if u in PLAIN else first_in_p
@@ -249,8 +258,6 @@
 
     for u in PLAIN:
         end_first(u)
-    pl.semaphore_wait(near4, 2)
-    signal(near_twin, twin)
     for u in PAIRED:
         end_first(u)
     for u in PLAIN:
@@ -273,20 +280,22 @@
             total = total + zrecv[k]
         return total
 
+    def spill(part, tile):
+        for p in range(2):
+            for k in range(part.shape[1] // 128):
+                at = p * 8 + tile + k
+                result[at : at + 1, :] = part[p : p + 1, k * 128 : (k + 1) * 128]
+
     plain = gather_z(zrecv0, z0_r)
-    result[0:2, 0:WIDE0] = plain
+    spill(plain, 0)
     paired = gather_z(zrecv1, z1_r)
-    result[0:2, WIDE0:1024] = paired
-
-    def spread(slots, slot, count, first, wrapped, target, s, r, value):
+    spill(paired, WIDE0 // 128)
+
+    def spread(slots, slot, targets, s, r, value):
         slots[slot] = value
-
-        def start(k, _):
-            push(slots.at[slot], slots.at[slot], s, r, target(wrapped(k)))
-            return 0
-
-        lax.fori_loop(first, first + count - 1, start, 0)
-        arrived = slots.at[pl.ds(0, count - 1)]
+        for target in targets:
+            push(slots.at[slot], slots.at[slot], s, r, target)
+        arrived = slots.at[pl.ds(0, len(targets))]
         pltpu.make_async_copy(arrived, arrived, r).wait()
         return jnp.sum(slots[...], axis=0)
 
@@ -295,14 +304,15 @@
         lanes = jnp.sum(part * part, axis=0, keepdims=True)
         for k in range(part.shape[1] // 128):
             square = square + lanes[:, k * 128 : (k + 1) * 128]
-    base = z * PLANE
-    square = spread(
-        plane_sum, q, PLANE, 1, lambda k: wrap(q + k, PLANE), lambda k: base + k, p_s, p_r, square
-    )
-    result[2:3, 0:128] = spread(
-        ring_sum, z, NZ, 8, lambda k: wrap(wrap(z + k + jnp.where(k >= NZ, 1, 0), NZ), NZ),
-        lambda k: k * PLANE + q, q_s, q_r, square,
-    )
+    away = [(j, i) for j in range(NY) for i in range(NX)]
+    away.sort(key=lambda k: -min(k[0], NY - k[0]) - min(k[1], NX - k[1]))
+    plane = [
+        device(z, wrap(y + j, NY), wrap(x + i, NX), c_)
+        for j, i in away for c_ in (1 - core, core) if j or i
+    ]
+    square = spread(plane_sum, q, plane + [twin], p_s, p_r, square)
+    ring = sorted(range(1, NZ), key=lambda k: -min(k, NZ - k))
+    result[16:17, :] = spread(ring_sum, z, [up(k) for k in ring], q_s, q_r, square)
 
     store = pltpu.make_async_copy(result, result_hbm, result_sem)
     store.start()
@@ -354,21 +364,19 @@
         load.start()
     for load in loads[:-1]:
         load.wait()
-    squares = jnp.sum(result[2:3, 0:128], axis=1, keepdims=True)
+    squares = jnp.sum(result[16:17, :], axis=1, keepdims=True)
     clip = jnp.minimum(1.0, 1.0 / jnp.sqrt(squares + 1e-12))
     scale_m, scale_v = sm[0], sv[0]
-    for p in range(2):
-        part = slice(p * 1024, (p + 1) * 1024)
-        m_old = scale_m * (cm[:, part].astype(jnp.float32) - 127.0) / 127.0
-        ratio_v = cv[:, part].astype(jnp.float32) / 255.0
-        v_old = scale_v * ratio_v * ratio_v
-        clipped = clip * result[p : p + 1, :]
-        m_new = 0.9 * m_old + 0.1 * clipped
-        v_new = 0.95 * v_old + 0.05 * clipped * clipped
-        update = m_new / (1.0 - 0.9**STEP) / (jnp.sqrt(v_new / (1.0 - 0.95**STEP)) + 1e-08)
-        nm[:, part] = ma[:, part] - 0.01 * (update + 0.1 * ma[:, part])
-        mu[:, part] = m_new / scale_m
-        vu[:, part] = v_new / scale_v
+    m_old = scale_m * (cm[...].astype(jnp.float32) - 127.0) / 127.0
+    ratio_v = cv[...].astype(jnp.float32) / 255.0
+    v_old = scale_v * ratio_v * ratio_v
+    clipped = clip * result[0:16, :]
+    m_new = 0.9 * m_old + 0.1 * clipped
+    v_new = 0.95 * v_old + 0.05 * clipped * clipped
+    update = m_new / (1.0 - 0.9**STEP) / (jnp.sqrt(v_new / (1.0 - 0.95**STEP)) + 1e-08)
+    nm[...] = ma[...] - 0.01 * (update + 0.1 * ma[...])
+    mu[...] = m_new / scale_m
+    vu[...] = v_new / scale_v
     for store in stores[1:]:
         store.start()
     loads[-1].wait()
@@ -382,24 +390,24 @@
     vmem, dma = pltpu.VMEM, pltpu.SemaphoreType.DMA
     shape = jax.ShapeDtypeStruct
     hbm = pl.BlockSpec(memory_space=pltpu.HBM)
-    block = shape((1, 2048), f32)
+    block = shape((16, 128), f32)
     d_attn, result = pl.pallas_call(
         kernel,
-        out_shape=(shape((TOK, 1024), bf16), shape((4, 1024), f32)),
+        out_shape=(shape((TOK, 1024), bf16), shape((24, 128), f32)),
         in_specs=[hbm] * 3,
         out_specs=(hbm,) * 2,
         scratch_shapes=[
             vmem((TOK, 1024), bf16),
-            vmem((4, 1024), f32),
+            vmem((24, 128), f32),
             vmem((TOK, 1024), bf16),
             vmem((TOK, 1024), bf16),
             vmem((1024, 1024), bf16),
             vmem((512, TOK), f32),
             vmem((512, TOK), f32),
-            vmem((4, TOK, 256), f32),
-            vmem((4, TOK, 256), f32),
             vmem((4, 4, 2, 16, 2 * TOK), bf16),
-            vmem((4, 2 * TOK, 256), bf16),
+            *[vmem((TOK, w), f32) for w in WIDTHS],
+            *[vmem((TOK, w), f32) for w in WIDTHS],
+            *[vmem((2 * TOK, w), bf16) for w in WIDTHS],
             vmem((4, 4, 32, WIDTHS[0]), f32),
             vmem((4, 4, 32, WIDTHS[1]), f32),
             vmem((4, 4, 16, WIDTHS[2]), f32),
@@ -436,28 +444,34 @@
             flops=2 * 2 * TOK * 1024 * 1024, bytes_accessed=3 * 2**20, transcendentals=0
         ),
     )(attn_out, grad_out, w_out)
-    return pl.pallas_call(
+    d_attn, m_unit, v_unit, new_master = pl.pallas_call(
         update_kernel,
         out_shape=(shape((TOK, 1024), bf16), block, block, block),
         in_specs=[hbm] * 7,
         out_specs=(hbm,) * 4,
         scratch_shapes=[
-            vmem((4, 1024), f32),
-            vmem((1, 2048), jnp.int32),
-            vmem((1, 2048), jnp.int32),
-            vmem((1, 2048), f32),
+            vmem((24, 128), f32),
+            vmem((16, 128), jnp.int32),
+            vmem((16, 128), jnp.int32),
+            vmem((16, 128), f32),
             pltpu.SMEM((1,), f32),
             pltpu.SMEM((1,), f32),
-            vmem((1, 2048), f32),
-            vmem((1, 2048), f32),
-            vmem((1, 2048), f32),
+            vmem((16, 128), f32),
+            vmem((16, 128), f32),
+            vmem((16, 128), f32),
             vmem((TOK, 1024), bf16),
             dma((7,)),
             dma((4,)),
         ],
         compiler_params=pltpu.CompilerParams(vmem_limit_bytes=60 * 2**20),
         cost_estimate=pl.CostEstimate(flops=2048 * 30, bytes_accessed=2**19, transcendentals=4096),
-    )(d_attn, result, codes_m, codes_v, master, scale_m, scale_v)
+    )(
+        d_attn, result, codes_m.reshape(16, 128), codes_v.reshape(16, 128),
+        master.reshape(16, 128), scale_m, scale_v,
+    )
+    return (
+        d_attn, m_unit.reshape(1, 2048), v_unit.reshape(1, 2048), new_master.reshape(1, 2048)
+    )
 
 
 def solution(mesh):

time: 54.8 us -> 53 us (0.967)
  Pallas kernels: 52.6 us -> 50.8 us
    pallas_call x1, Pallas kernels: 50.8 us -> 49 us  [local(): pl.pallas_call(kernel, out_shape=(shape((TOK, 1024), bf16), shape((24, 12...]
where the time goes in v4:
time: 53 us; the launch traced here: 52.8 us
  Pallas kernels  50.8 us (96%)
  between operations  1.93 us (4%)
    pallas_call x1, Pallas kernels, local(): pl.pallas_call(kernel, out_shape=(shape((TOK, 1024), bf16), shape((24, 12...  49 us
    pallas_call x1, Pallas kernels, local(): pl.pallas_call(update_kernel, out_shape=(shape((TOK, 1024), bf16), block,...  1.82 us

profile of v4, /device:TPU:1, one launch (start us, length us, event | category | flops | bytes accessed | tf_op | source)
XLA Modules:
  0.0 52.8 jit_solution(2038064708284457170)
XLA Ops:
  1.9 49.0 %shard_map.111 = (bf16[128,1024]{1,0:T(8,128)(2,1)}, f32[24,128]{1,0:T(8,128)}) custom-call(bf16[128,1024]{1,0:T(8,128)(2,1)} %a_hbm.1, bf16[128,1024]{1,0:T(8,128)(2,1)} %g_hbm.1, bf16[1024,1024]{1,0:T(8,128)(2,1)} %w_hbm.1), custom_call_target="tpu_custom_call" | custom-call | flops 536870912 | bytes 3145728 | tf_op jit(solution)/shard_map/pallas_call | solution.py:394
  50.9 1.8 %shard_map.112 = (bf16[128,1024]{1,0:T(8,128)(2,1)}, f32[16,128]{1,0:T(8,128)}, f32[16,128]{1,0:T(8,128)}, f32[16,128]{1,0:T(8,128)}) custom-call(bf16[128,1024]{1,0:T(8,128)(2,1)} %get-tuple-element.10.d_hbm, f32[24,128]{1,0:T(8,128)} %get-tuple-element.11.result_hbm, s32[16,128]{1,0:T(8,128)} %bitcast.6, s32[16,128]{1,0:T(8,128)} %bitcast.7, ...), custom_call_target="tpu_custom_call" | custom-call | flops 61440 | bytes 524288 | tf_op jit(solution)/shard_map/pallas_call | solution.py:447

commit v5 on v4

--- a/solution.py
+++ b/solution.py
@@ -11,6 +11,7 @@
 NX, NY, NZ = 4, 4, 16
 PLANE = NX * NY * 2
 TOK = 128
+VMEM = int(53.5 * 2**20)
 WIDTHS = (256, 256, 256, 256)
 STARTS = tuple(sum(WIDTHS[:u]) for u in range(4))
 PLAIN, PAIRED = (0, 1), (2, 3)
@@ -33,14 +34,14 @@
 
 def kernel(
     a_hbm, g_hbm, w_hbm,
-    d_hbm, result_hbm,
-    d_ref, result, a_in, g_in, w_in,
+    d_ref, result,
+    a_in, g_in, w_in,
     at_send, at_recv, at_all,
     gs0, gs1, gs2, gs3, gr0, gr1, gr2, gr3, ga0, ga1, ga2, ga3,
     prod0, prod1, prod2, prod3, pair, pair_in, first_in, first_in_p, second_in, second_in_p,
     zsend0, zrecv0, zsend1, zrecv1, plane_sum, ring_sum,
     in_sem, core_s, core_r, pair_s, pair_r, first_s, first_r, second_s, second_r,
-    z0_s, z0_r, z1_s, z1_r, p_s, p_r, q_s, q_r, d_sem, result_sem,
+    z0_s, z0_r, z1_s, z1_r, p_s, p_r, q_s, q_r,
     order, near1, near2, near4, near_twin,
 ):
     me = lax.axis_index("dp")
@@ -48,7 +49,6 @@
     x = lax.rem(me // 2, NX)
     y = lax.rem(me // (2 * NX), NY)
     z = me // PLANE
-    q = lax.rem(me, PLANE)
     parity = lax.rem(z, 2)
 
     def device(z_, y_, x_, c_):
@@ -106,12 +106,11 @@
         g_all[u][0:TOK, :] = piece
 
     loads[0].wait()
-    for u in PLAIN:
-        cross(u)
+    cross(0)
     loads[1].wait()
     at_send[...] = rows_of(1 - core)
     across[4] = push(at_send, at_recv, core_s.at[4], core_r.at[4], twin)
-    for u in PAIRED:
+    for u in range(1, 4):
         cross(u)
     signal(near1, up(1), up(NZ - 1))
 
@@ -202,8 +201,6 @@
     loads[2].wait()
     for h in range(4):
         cotangent(h)
-    d_store = pltpu.make_async_copy(d_ref, d_hbm, d_sem)
-    d_store.start()
     pl.semaphore_wait(near4, 2)
     signal(near_twin, twin)
 
@@ -295,9 +292,15 @@
         slots[slot] = value
         for target in targets:
             push(slots.at[slot], slots.at[slot], s, r, target)
-        arrived = slots.at[pl.ds(0, len(targets))]
+
+    def collect(slots, count, r):
+        arrived = slots.at[pl.ds(0, count)]
         pltpu.make_async_copy(arrived, arrived, r).wait()
         return jnp.sum(slots[...], axis=0)
+
+    def left(buffer, count, s):
+        gone = buffer.at[pl.ds(0, count)]
+        pltpu.make_async_copy(gone, gone, s).wait()
 
     square = jnp.zeros((1, 128), jnp.float32)
     for part in (plain, paired):
@@ -309,23 +312,16 @@
     plane = [
         device(z, wrap(y + j, NY), wrap(x + i, NX), c_)
         for j, i in away for c_ in (1 - core, core) if j or i
-    ]
-    square = spread(plane_sum, q, plane + [twin], p_s, p_r, square)
-    ring = sorted(range(1, NZ), key=lambda k: -min(k, NZ - k))
-    result[16:17, :] = spread(ring_sum, z, [up(k) for k in ring], q_s, q_r, square)
-
-    store = pltpu.make_async_copy(result, result_hbm, result_sem)
-    store.start()
-    store.wait()
-    d_store.wait()
-    for sent in (across, sent_pair, sent_first, sent_second):
+    ] + [twin]
+    spread(plane_sum, (y * NX + x) * 2 + core, plane, p_s, p_r, square)
+    for sent in (across, sent_pair, sent_first):
         for copy in sent.values():
             copy.wait_send()
-
-    def left(buffer, count, s):
-        gone = buffer.at[pl.ds(0, count)]
-        pltpu.make_async_copy(gone, gone, s).wait()
-
+    square = collect(plane_sum, PLANE - 1, p_r)
+    offsets = sorted(range(1, NZ), key=lambda k: -min(k, NZ - k))
+    spread(ring_sum, z, [up(k) for k in offsets], q_s, q_r, square)
+    for copy in sent_second.values():
+        copy.wait_send()
     at_home = (z // 8) == core
 
     @pl.when(at_home)
@@ -339,31 +335,18 @@
         left(zsend1, 8, z1_s)
 
     left(plane_sum, PLANE - 1, p_s)
+    result[16:17, :] = collect(ring_sum, NZ - 1, q_r)
     left(ring_sum, NZ - 1, q_s)
 
 
 def update_kernel(
-    d_hbm, result_hbm, cm_hbm, cv_hbm, ma_hbm, sm_hbm, sv_hbm,
-    d_out, mu_out, vu_out, nm_out,
-    result, cm, cv, ma, sm, sv, mu, vu, nm, d, load_sem, store_sem,
+    d, result, cm, cv, ma, sm, sv, d_out, mu_out, vu_out, nm_out, mu, vu, nm, store_sem
 ):
     stores = [
         pltpu.make_async_copy(src, dst, store_sem.at[i])
         for i, (src, dst) in enumerate(((d, d_out), (mu, mu_out), (vu, vu_out), (nm, nm_out)))
     ]
-    loads = [
-        pltpu.make_async_copy(src, dst, load_sem.at[i])
-        for i, (src, dst) in enumerate(
-            (
-                (result_hbm, result), (cm_hbm, cm), (cv_hbm, cv), (ma_hbm, ma),
-                (sm_hbm, sm), (sv_hbm, sv), (d_hbm, d),
-            )
-        )
-    ]
-    for load in loads:
-        load.start()
-    for load in loads[:-1]:
-        load.wait()
+    stores[0].start()
     squares = jnp.sum(result[16:17, :], axis=1, keepdims=True)
     clip = jnp.minimum(1.0, 1.0 / jnp.sqrt(squares + 1e-12))
     scale_m, scale_v = sm[0], sv[0]
@@ -379,8 +362,6 @@
     vu[...] = v_new / scale_v
     for store in stores[1:]:
         store.start()
-    loads[-1].wait()
-    stores[0].start()
     for store in stores:
         store.wait()
 
@@ -389,16 +370,16 @@
     f32, bf16 = jnp.float32, jnp.bfloat16
     vmem, dma = pltpu.VMEM, pltpu.SemaphoreType.DMA
     shape = jax.ShapeDtypeStruct
+    near = pl.BlockSpec(memory_space=pltpu.VMEM)
+    scalar = pl.BlockSpec(memory_space=pltpu.SMEM)
     hbm = pl.BlockSpec(memory_space=pltpu.HBM)
     block = shape((16, 128), f32)
     d_attn, result = pl.pallas_call(
         kernel,
         out_shape=(shape((TOK, 1024), bf16), shape((24, 128), f32)),
         in_specs=[hbm] * 3,
-        out_specs=(hbm,) * 2,
+        out_specs=(near,) * 2,
         scratch_shapes=[
-            vmem((TOK, 1024), bf16),
-            vmem((24, 128), f32),
             vmem((TOK, 1024), bf16),
             vmem((TOK, 1024), bf16),
             vmem((1024, 1024), bf16),
@@ -433,12 +414,12 @@
             dma((4, 3)),
             dma((4, 3)),
             dma((4, 3)),
-            *[dma] * 10,
+            *[dma] * 8,
             vmem((512, 512), bf16),
             *[pltpu.SemaphoreType.REGULAR] * 4,
         ],
         compiler_params=pltpu.CompilerParams(
-            collective_id=0, has_side_effects=True, vmem_limit_bytes=60 * 2**20
+            collective_id=0, has_side_effects=True, vmem_limit_bytes=VMEM
         ),
         cost_estimate=pl.CostEstimate(
             flops=2 * 2 * TOK * 1024 * 1024, bytes_accessed=3 * 2**20, transcendentals=0
@@ -447,23 +428,15 @@
     d_attn, m_unit, v_unit, new_master = pl.pallas_call(
         update_kernel,
         out_shape=(shape((TOK, 1024), bf16), block, block, block),
-        in_specs=[hbm] * 7,
+        in_specs=[near] * 5 + [scalar] * 2,
         out_specs=(hbm,) * 4,
         scratch_shapes=[
-            vmem((24, 128), f32),
-            vmem((16, 128), jnp.int32),
-            vmem((16, 128), jnp.int32),
-            vmem((16, 128), f32),
-            pltpu.SMEM((1,), f32),
-            pltpu.SMEM((1,), f32),
             vmem((16, 128), f32),
             vmem((16, 128), f32),
             vmem((16, 128), f32),
-            vmem((TOK, 1024), bf16),
-            dma((7,)),
             dma((4,)),
         ],
-        compiler_params=pltpu.CompilerParams(vmem_limit_bytes=60 * 2**20),
+        compiler_params=pltpu.CompilerParams(vmem_limit_bytes=VMEM),
         cost_estimate=pl.CostEstimate(flops=2048 * 30, bytes_accessed=2**19, transcendentals=4096),
     )(
         d_attn, result, codes_m.reshape(16, 128), codes_v.reshape(16, 128),

time: 53 us -> 51.3 us (0.968)
  Pallas kernels: 50.8 us -> 49.1 us
    pallas_call x1, Pallas kernels: 1.82 us -> 0.76 us  [local(): pl.pallas_call(update_kernel, out_shape=(shape((TOK, 1024), bf16), block,...]
    pallas_call x1, Pallas kernels: 49 us -> 48.3 us  [local(): pl.pallas_call(kernel, out_shape=(shape((TOK, 1024), bf16), shape((24, 12...]
where the time goes in v5:
time: 51.3 us; the launch traced here: 51.1 us
  Pallas kernels  49.1 us (96%)
  between operations  2 us (4%)
    pallas_call x1, Pallas kernels, local(): pl.pallas_call(kernel, out_shape=(shape((TOK, 1024), bf16), shape((24, 12...  48.3 us

profile of v5, /device:TPU:1, one launch (start us, length us, event | category | flops | bytes accessed | tf_op | source)
XLA Modules:
  0.0 51.1 jit_solution(17972121796808061896)
XLA Ops:
  0.6 0.0 copy-start.2
  0.6 0.0 copy-start.1
  0.7 0.0 copy-start
  2.0 48.3 %shard_map.111 = (bf16[128,1024]{1,0:T(8,128)(2,1)S(1)}, f32[24,128]{1,0:T(8,128)S(1)}) custom-call(bf16[128,1024]{1,0:T(8,128)(2,1)} %a_hbm.1, bf16[128,1024]{1,0:T(8,128)(2,1)} %g_hbm.1, bf16[1024,1024]{1,0:T(8,128)(2,1)} %w_hbm.1), custom_call_target="tpu_custom_call" | custom-call | flops 536870912 | bytes 3145728 | tf_op jit(solution)/shard_map/pallas_call | solution.py:377
  50.3 0.0 copy-done.2
  50.3 0.0 copy-done.1
  50.3 0.0 copy-done
  50.4 0.8 %shard_map.112 = (bf16[128,1024]{1,0:T(8,128)(2,1)}, f32[16,128]{1,0:T(8,128)}, f32[16,128]{1,0:T(8,128)}, f32[16,128]{1,0:T(8,128)}) custom-call(bf16[128,1024]{1,0:T(8,128)(2,1)S(1)} %get-tuple-element.10.d, f32[24,128]{1,0:T(8,128)S(1)} %get-tuple-element.11.result, s32[16,128]{1,0:T(8,128)S(1)} %bitcast.6, s32[16,128]{1,0:T(8,128)S(1)} %bitcast.7, ...), custom_call_target="tpu_custom_call" | custom-call | flops 61440 | bytes 524288 | tf_op jit(solution)/shard_map/pallas_call | solution.py:428
Async XLA Ops:
  0.6 49.7 %copy-start.2 = (f32[1,2048]{1,0:T(1,128)S(1)}, f32[1,2048]{1,0:T(1,128)}, u32[]{:S(2)}) copy-start(f32[1,2048]{1,0:T(1,128)} %param.15) | copy-start | bytes 24580
  0.6 49.7 %copy-start.1 = (s32[1,2048]{1,0:T(1,128)S(1)}, s32[1,2048]{1,0:T(1,128)}, u32[]{:S(2)}) copy-start(s32[1,2048]{1,0:T(1,128)} %param.12) | copy-start | bytes 24580
  0.7 49.7 %copy-start = (s32[1,2048]{1,0:T(1,128)S(1)}, s32[1,2048]{1,0:T(1,128)}, u32[]{:S(2)}) copy-start(s32[1,2048]{1,0:T(1,128)} %param.11) | copy-start | bytes 24580

commit v6 on v5

--- a/solution.py
+++ b/solution.py
@@ -198,11 +198,6 @@
             prod[u][hop] = prod[u][hop] + pair_in[u - 2, hop]
             send_first(u, hop)
 
-    loads[2].wait()
-    for h in range(4):
-        cotangent(h)
-    pl.semaphore_wait(near4, 2)
-    signal(near_twin, twin)
 
     def end_first(u):
         into = first_in if u in PLAIN else first_in_p
@@ -255,6 +250,8 @@
 
     for u in PLAIN:
         end_first(u)
+    pl.semaphore_wait(near4, 2)
+    signal(near_twin, twin)
     for u in PAIRED:
         end_first(u)
     for u in PLAIN:
@@ -320,6 +317,9 @@
     square = collect(plane_sum, PLANE - 1, p_r)
     offsets = sorted(range(1, NZ), key=lambda k: -min(k, NZ - k))
     spread(ring_sum, z, [up(k) for k in offsets], q_s, q_r, square)
+    loads[2].wait()
+    for h in range(4):
+        cotangent(h)
     for copy in sent_second.values():
         copy.wait_send()
     at_home = (z // 8) == core

time: 51.3 us -> 51 us (level)
  no operation moved by 1% of the time
where the time goes in v6:
time: 51 us; the launch traced here: 50.9 us
  Pallas kernels  48.8 us (96%)
  between operations  2 us (4%)
    pallas_call x1, Pallas kernels, local(): pl.pallas_call(kernel, out_shape=(shape((TOK, 1024), bf16), shape((24, 12...  48.1 us

profile of v6, /device:TPU:1, one launch (start us, length us, event | category | flops | bytes accessed | tf_op | source)
XLA Modules:
  0.0 50.9 jit_solution(1610903768035750599)
XLA Ops:
  0.6 0.0 copy-start.2
  0.6 0.0 copy-start.1
  0.7 0.0 copy-start
  2.0 48.1 %shard_map.111 = (bf16[128,1024]{1,0:T(8,128)(2,1)S(1)}, f32[24,128]{1,0:T(8,128)S(1)}) custom-call(bf16[128,1024]{1,0:T(8,128)(2,1)} %a_hbm.1, bf16[128,1024]{1,0:T(8,128)(2,1)} %g_hbm.1, bf16[1024,1024]{1,0:T(8,128)(2,1)} %w_hbm.1), custom_call_target="tpu_custom_call" | custom-call | flops 536870912 | bytes 3145728 | tf_op jit(solution)/shard_map/pallas_call | solution.py:377
  50.1 0.0 copy-done.2
  50.1 0.0 copy-done.1
  50.1 0.0 copy-done
  50.1 0.8 %shard_map.112 = (bf16[128,1024]{1,0:T(8,128)(2,1)}, f32[16,128]{1,0:T(8,128)}, f32[16,128]{1,0:T(8,128)}, f32[16,128]{1,0:T(8,128)}) custom-call(bf16[128,1024]{1,0:T(8,128)(2,1)S(1)} %get-tuple-element.10.d, f32[24,128]{1,0:T(8,128)S(1)} %get-tuple-element.11.result, s32[16,128]{1,0:T(8,128)S(1)} %bitcast.6, s32[16,128]{1,0:T(8,128)S(1)} %bitcast.7, ...), custom_call_target="tpu_custom_call" | custom-call | flops 61440 | bytes 524288 | tf_op jit(solution)/shard_map/pallas_call | solution.py:428
Async XLA Ops:
  0.6 49.4 %copy-start.2 = (f32[1,2048]{1,0:T(1,128)S(1)}, f32[1,2048]{1,0:T(1,128)}, u32[]{:S(2)}) copy-start(f32[1,2048]{1,0:T(1,128)} %param.15) | copy-start | bytes 24580
  0.6 49.4 %copy-start.1 = (s32[1,2048]{1,0:T(1,128)S(1)}, s32[1,2048]{1,0:T(1,128)}, u32[]{:S(2)}) copy-start(s32[1,2048]{1,0:T(1,128)} %param.12) | copy-start | bytes 24580
  0.7 49.4 %copy-start = (s32[1,2048]{1,0:T(1,128)S(1)}, s32[1,2048]{1,0:T(1,128)}, u32[]{:S(2)}) copy-start(s32[1,2048]{1,0:T(1,128)} %param.11) | copy-start | bytes 24580

commit v7 on v6

--- a/solution.py
+++ b/solution.py
@@ -282,8 +282,12 @@
 
     plain = gather_z(zrecv0, z0_r)
     spill(plain, 0)
+    def squares_of(part):
+        lanes = jnp.sum(part * part, axis=0, keepdims=True)
+        return sum(lanes[:, k * 128 : (k + 1) * 128] for k in range(part.shape[1] // 128))
+
+    square = squares_of(plain)
     paired = gather_z(zrecv1, z1_r)
-    spill(paired, WIDE0 // 128)
 
     def spread(slots, slot, targets, s, r, value):
         slots[slot] = value
@@ -299,11 +303,7 @@
         gone = buffer.at[pl.ds(0, count)]
         pltpu.make_async_copy(gone, gone, s).wait()
 
-    square = jnp.zeros((1, 128), jnp.float32)
-    for part in (plain, paired):
-        lanes = jnp.sum(part * part, axis=0, keepdims=True)
-        for k in range(part.shape[1] // 128):
-            square = square + lanes[:, k * 128 : (k + 1) * 128]
+    square = square + squares_of(paired)
     away = [(j, i) for j in range(NY) for i in range(NX)]
     away.sort(key=lambda k: -min(k[0], NY - k[0]) - min(k[1], NX - k[1]))
     plane = [
@@ -311,6 +311,7 @@
         for j, i in away for c_ in (1 - core, core) if j or i
     ] + [twin]
     spread(plane_sum, (y * NX + x) * 2 + core, plane, p_s, p_r, square)
+    spill(paired, WIDE0 // 128)
     for sent in (across, sent_pair, sent_first):
         for copy in sent.values():
             copy.wait_send()

time: 51 us -> 51 us (level)
  no operation moved by 1% of the time
where the time goes in v7:
time: 51 us; the launch traced here: 50.9 us
  Pallas kernels  48.8 us (96%)
  between operations  2 us (4%)
    pallas_call x1, Pallas kernels, local(): pl.pallas_call(kernel, out_shape=(shape((TOK, 1024), bf16), shape((24, 12...  48.1 us

profile of v7, /device:TPU:1, one launch (start us, length us, event | category | flops | bytes accessed | tf_op | source)
XLA Modules:
  0.0 50.9 jit_solution(13173762900027526244)
XLA Ops:
  0.6 0.0 copy-start.2
  0.6 0.0 copy-start.1
  0.7 0.0 copy-start
  2.0 48.1 %shard_map.111 = (bf16[128,1024]{1,0:T(8,128)(2,1)S(1)}, f32[24,128]{1,0:T(8,128)S(1)}) custom-call(bf16[128,1024]{1,0:T(8,128)(2,1)} %a_hbm.1, bf16[128,1024]{1,0:T(8,128)(2,1)} %g_hbm.1, bf16[1024,1024]{1,0:T(8,128)(2,1)} %w_hbm.1), custom_call_target="tpu_custom_call" | custom-call | flops 536870912 | bytes 3145728 | tf_op jit(solution)/shard_map/pallas_call | solution.py:378
  50.1 0.0 copy-done.2
  50.1 0.0 copy-done.1
  50.1 0.0 copy-done
  50.1 0.8 %shard_map.112 = (bf16[128,1024]{1,0:T(8,128)(2,1)}, f32[16,128]{1,0:T(8,128)}, f32[16,128]{1,0:T(8,128)}, f32[16,128]{1,0:T(8,128)}) custom-call(bf16[128,1024]{1,0:T(8,128)(2,1)S(1)} %get-tuple-element.10.d, f32[24,128]{1,0:T(8,128)S(1)} %get-tuple-element.11.result, s32[16,128]{1,0:T(8,128)S(1)} %bitcast.6, s32[16,128]{1,0:T(8,128)S(1)} %bitcast.7, ...), custom_call_target="tpu_custom_call" | custom-call | flops 61440 | bytes 524288 | tf_op jit(solution)/shard_map/pallas_call | solution.py:429
Async XLA Ops:
  0.6 49.4 %copy-start.2 = (f32[1,2048]{1,0:T(1,128)S(1)}, f32[1,2048]{1,0:T(1,128)}, u32[]{:S(2)}) copy-start(f32[1,2048]{1,0:T(1,128)} %param.15) | copy-start | bytes 24580
  0.6 49.4 %copy-start.1 = (s32[1,2048]{1,0:T(1,128)S(1)}, s32[1,2048]{1,0:T(1,128)}, u32[]{:S(2)}) copy-start(s32[1,2048]{1,0:T(1,128)} %param.12) | copy-start | bytes 24580
  0.7 49.4 %copy-start = (s32[1,2048]{1,0:T(1,128)S(1)}, s32[1,2048]{1,0:T(1,128)}, u32[]{:S(2)}) copy-start(s32[1,2048]{1,0:T(1,128)} %param.11) | copy-start | bytes 24580
